TPU v7x, 32 devices: a whole 2x2x4 slice. The times are simulated.
32 devices in a mesh: dp: 4 (over y, core), expert: 8 (over z, x).
Axes of the slice: x: 2, y: 2, z: 4, core: 2. Of those that a mesh axis runs over, the one named last changes fastest.
Arguments:
- tokens: bfloat16 [4096, 2048], P(('dp', 'expert')), may hold values from -6 to 6
- out_grad: bfloat16 [4096, 2048], P(('dp', 'expert')), may hold values from -6 to 6
- route_ids: int32 [4096, 2], P(('dp', 'expert')), may hold values from 0 to 7, as said below
- route_gates: bfloat16 [4096, 2], P(('dp', 'expert')), may hold values from 0.049804688 to 1
- weight_in: bfloat16 [8, 2048, 512], P('expert', 'dp'), may hold values from -0.125 to 0.125
- weight_out: bfloat16 [8, 512, 2048], P('expert', None, 'dp'), may hold values from -0.25 to 0.25
Outputs:
- grad_tokens: bfloat16 [4096, 2048], P(('dp', 'expert'))
- grad_gates: bfloat16 [4096, 2], P(('dp', 'expert'))
- grad_weight_in: float32 [8, 2048, 512], P('expert', 'dp')
- grad_weight_out: float32 [8, 512, 2048], P('expert', None, 'dp')
Inputs may be any that keep to these rules, and one draw needn't show every extreme that they name: `route_ids`: each row names two different experts. Within the 128 tokens of one device (aligned blocks of 128 rows), every expert is named by at most 64 rows. For each index of dp, one expert is named by exactly 64 rows in every block of that index's 1024 rows.
All inputs are finite; a program needn't handle non-finite values.
Results may differ from a plain program's by a relative error of at most 0.017.
Values may be sent and summed in bfloat16 or wider, within the bound.
No kernel may reach another device: no remote copies, remote signals or barrier semaphores. Data moves between devices by JAX's collectives and lax.ppermute only.
A program may use at most 64 MiB of HBM per device.

v0:
```python
import jax
import jax.numpy as jnp
from jax import lax
from jax.sharding import PartitionSpec as P


def silu_slope(preact):
    logistic = jax.nn.sigmoid(preact)
    return logistic * (1.0 + preact * (1.0 - logistic))


def forward_rows(inputs, full_in):
    preact = jnp.dot(inputs, full_in, preferred_element_type=jnp.float32)
    return (preact, jax.nn.silu(preact).astype(jnp.bfloat16))


def backward_rows(inputs, grad_rows, gate_rows, preact, hidden_act, full_in, full_out):
    back_grad = lax.dot_general(
        grad_rows, full_out, (((1,), (1,)), ((), ())), preferred_element_type=jnp.float32
    )
    weight = gate_rows.astype(jnp.float32)[:, None]
    gate_grad = jnp.sum(hidden_act.astype(jnp.float32) * back_grad, axis=1)
    pre_grad = (weight * back_grad * silu_slope(preact)).astype(jnp.bfloat16)
    scaled = (weight * grad_rows.astype(jnp.float32)).astype(jnp.bfloat16)
    route_grad = lax.dot_general(
        pre_grad, full_in, (((1,), (1,)), ((), ())), preferred_element_type=jnp.float32
    ).astype(jnp.bfloat16)
    term_in = lax.dot_general(
        inputs, pre_grad, (((0,), (0,)), ((), ())), preferred_element_type=jnp.float32
    )
    term_out = lax.dot_general(
        hidden_act, scaled, (((0,), (0,)), ((), ())), preferred_element_type=jnp.float32
    )
    return (route_grad, gate_grad, term_in, term_out)


def on_device(tokens, out_grad, route_ids, route_gates, weight_in, weight_out):
    local_tokens, model_width = tokens.shape
    experts = lax.axis_size("expert")
    capacity = 4 * local_tokens // experts
    slot_count = experts * capacity
    full_in, full_out = (
        lax.all_gather(weight_in, "dp", axis=1, tiled=True),
        lax.all_gather(weight_out, "dp", axis=2, tiled=True),
    )
    full_in = full_in[0]
    full_out = full_out[0]
    flat_ids = route_ids.reshape(-1)
    onehot = (flat_ids[:, None] == jnp.arange(experts, dtype=jnp.int32)[None, :]).astype(jnp.int32)
    route_rank = jnp.sum(jnp.cumsum(onehot, axis=0) * onehot, axis=1) - 1
    slot_index = flat_ids * capacity + route_rank
    route_count = 2 * local_tokens
    route_of_slot = (
        jnp.full((slot_count,), route_count, jnp.int32)
        .at[slot_index]
        .set(jnp.arange(route_count, dtype=jnp.int32))
    )
    token_of_slot = route_of_slot // 2
    outbound_inputs = jnp.take(tokens, token_of_slot, axis=0, mode="fill", fill_value=0)
    outbound_grads = jnp.take(out_grad, token_of_slot, axis=0, mode="fill", fill_value=0)
    outbound_gates = jnp.take(
        route_gates.reshape(-1), route_of_slot, axis=0, mode="fill", fill_value=0
    )
    arrived_inputs, arrived_grads, arrived_gates = (
        lax.all_to_all(outbound_inputs, "expert", split_axis=0, concat_axis=0, tiled=True),
        lax.all_to_all(outbound_grads, "expert", split_axis=0, concat_axis=0, tiled=True),
        lax.all_to_all(outbound_gates, "expert", split_axis=0, concat_axis=0, tiled=True),
    )
    preact, hidden_act = forward_rows(arrived_inputs, full_in)
    back_rows, back_gates, sum_in, sum_out = backward_rows(
        arrived_inputs, arrived_grads, arrived_gates, preact, hidden_act, full_in, full_out
    )
    home_grads, home_gates = (
        lax.all_to_all(back_rows, "expert", split_axis=0, concat_axis=0, tiled=True),
        lax.all_to_all(
            back_gates.astype(jnp.bfloat16), "expert", split_axis=0, concat_axis=0, tiled=True
        ),
    )
    pair_rows = home_grads[slot_index].reshape(local_tokens, 2, model_width)
    grad_tokens = (
        pair_rows[:, 0].astype(jnp.float32) + pair_rows[:, 1].astype(jnp.float32)
    ).astype(jnp.bfloat16)
    grad_gates = home_gates[slot_index].reshape(local_tokens, 2)
    grad_weight_in, grad_weight_out = (
        lax.psum_scatter(
            sum_in[None].astype(jnp.bfloat16), "dp", scatter_dimension=1, tiled=True
        ).astype(jnp.float32),
        lax.psum_scatter(
            sum_out[None].astype(jnp.bfloat16), "dp", scatter_dimension=2, tiled=True
        ).astype(jnp.float32),
    )
    return (grad_tokens, grad_gates, grad_weight_in, grad_weight_out)


def solution(mesh):
    return jax.shard_map(
        on_device,
        mesh=mesh,
        in_specs=(
            P(("dp", "expert"), None),
            P(("dp", "expert"), None),
            P(("dp", "expert"), None),
            P(("dp", "expert"), None),
            P("expert", "dp", None),
            P("expert", None, "dp"),
        ),
        out_specs=(
            P(("dp", "expert"), None),
            P(("dp", "expert"), None),
            P("expert", "dp", None),
            P("expert", None, "dp"),
        ),
        check_vma=False,
    )
```

profile of v0, /device:TPU:0, one launch (start us, length us, event | category | flops | bytes accessed | tf_op | source)
XLA Modules:
  0.0 227.0 jit_solution(9825531673572937889)
XLA Ops:
  7.2 0.8 copy.20
  8.3 0.7 broadcast_multiply_fusion
  10.2 1.4 scatter_custom_fusion
  11.6 0.8 copy.22
  12.6 3.4 %gather_fusion = bf16[512]{0:T(512)(128)(2,1)S(1)} fusion(bf16[256]{0:T(256)(128)(2,1)S(1)} %reshape.132, s32[1024]{0:T(1024)S(1)} %pad_clamp_fusion.2), kind=kCustom, calls=%fused_computation.2 | custom fusion | bytes 4096 | tf_op jit(solution)/shard_map/jit(_take)/gather | solution.py:61
  16.6 7.3 %all-to-all-start = ((bf16[8,64,1]{1,2,0:T(2,128)(2,1)}), bf16[8,64,1]{1,2,0:T(2,128)(2,1)S(1)}, u32[]{:S(2)}, u32[]{:S(2)}) async-start(bf16[8,64,1]{1,2,0:T(2,128)(2,1)} %select_n.52), calls=%async_computation | async-start | bytes 8192 | tf_op jit(solution)/shard_map/all_to_all | solution.py:67
  23.9 2.5 %gather_fusion.3 = bf16[512,2048]{1,0:T(8,128)(2,1)S(1)} fusion(bf16[128,2048]{1,0:T(8,128)(2,1)S(1)} %copy-done, s32[1024]{0:T(1024)S(1)} %pad_clamp_fusion.1), kind=kCustom, calls=%fused_computation.clone | custom fusion | bytes 4196352 | tf_op jit(solution)/shard_map/jit(_take)/gather | solution.py:60
  26.4 3.3 %gather_fusion.4 = bf16[512,2048]{1,0:T(8,128)(2,1)} fusion(bf16[128,2048]{1,0:T(8,128)(2,1)S(1)} %copy-done.1, s32[1024]{0:T(1024)S(1)} %pad_clamp_fusion.1), kind=kCustom, calls=%fused_computation.1.clone | custom fusion | bytes 4196352 | tf_op jit(solution)/shard_map/jit(_take)/gather | solution.py:59
  29.7 3.9 %broadcast_select_fusion.1 = (bf16[512,2048]{1,0:T(8,128)(2,1)}, bf16[512,2048]{1,0:T(8,128)(2,1)}) fusion(bf16[512,2048]{1,0:T(8,128)(2,1)S(1)} %gather_fusion.3, pred[512]{0:T(512)(128)(4,1)S(1)} %get-tuple-element.13, bf16[512,2048]{1,0:T(8,128)(2,1)} %gather_fusion.4), kind=kLoop, calls=%fused_computation.19 | loop fusion | flops 2097152 | bytes 8389120 | tf_op jit(solution)/shard_map/jit(_take)/select_n | solution.py:60
  33.6 6.0 %all-to-all-start.2 = ((bf16[8,64,2048]{2,1,0:T(8,128)(2,1)}), bf16[8,64,2048]{2,1,0:T(8,128)(2,1)S(1)}, u32[]{:S(2)}, u32[]{:S(2)}) async-start(bf16[8,64,2048]{2,1,0:T(8,128)(2,1)} %bitcast.36), calls=%async_computation.2 | async-start | bytes 4194304 | tf_op jit(solution)/shard_map/all_to_all | solution.py:65
  40.4 46.9 %all-to-all-done.2 = bf16[8,64,2048]{2,1,0:T(8,128)(2,1)S(1)} async-done(((bf16[8,64,2048]{2,1,0:T(8,128)(2,1)}), bf16[8,64,2048]{2,1,0:T(8,128)(2,1)S(1)}, u32[]{:S(2)}, u32[]{:S(2)}) %all-to-all-start.2) | async-done | bytes 2097184 | tf_op jit(solution)/shard_map/all_to_all | solution.py:65
  87.3 1.3 copy-done.3
  88.6 3.6 %all-to-all-start.1 = ((bf16[8,64,2048]{2,1,0:T(8,128)(2,1)}), bf16[8,64,2048]{2,1,0:T(8,128)(2,1)S(1)}, u32[]{:S(2)}, u32[]{:S(2)}) async-start(bf16[8,64,2048]{2,1,0:T(8,128)(2,1)} %bitcast.4), calls=%async_computation.1 | async-start | bytes 4194304 | tf_op jit(solution)/shard_map/all_to_all | solution.py:66
  92.3 0.7 all-gather.3.cloned.1.call-update
  93.1 4.5 %fusion.3 = f32[512,512]{0,1:T(8,128)} fusion(bf16[512,2048]{1,0:T(8,128)(2,1)} %bitcast.39, bf16[1,2048,512]{2,1,0:T(8,128)(2,1)} %all-gather.5.cloned.1.call-done), kind=kOutput, calls=%fused_computation.13 | convolution fusion | flops 1073741824 | bytes 5242880 | tf_op jit(solution)/shard_map/dot_general | solution.py:13
  97.6 21.1 %all-gather.3.cloned.1.call-done = bf16[1,512,2048]{2,1,0:T(8,128)(2,1)} async-done(((bf16[1,512,512]{2,1,0:T(8,128)(2,1)}), bf16[1,512,2048]{2,1,0:T(8,128)(2,1)}) %all-gather.3.cloned.1.call-update) | async-done | bytes 2097168 | tf_op jit(solution)/shard_map/all_gather | solution.py:44
  118.7 22.0 %all-to-all-done.1 = bf16[8,64,2048]{2,1,0:T(8,128)(2,1)S(1)} async-done(((bf16[8,64,2048]{2,1,0:T(8,128)(2,1)}), bf16[8,64,2048]{2,1,0:T(8,128)(2,1)S(1)}, u32[]{:S(2)}, u32[]{:S(2)}) %all-to-all-start.1) | async-done | bytes 2097184 | tf_op jit(solution)/shard_map/all_to_all | solution.py:66
  140.7 4.3 %multiply_reduce_fusion = (bf16[512]{0:T(512)(128)(2,1)S(1)}, bf16[512,512]{0,1:T(8,128)(2,1)S(1)}) fusion(f32[512,512]{0,1:T(8,128)} %fusion.3, f32[512]{0:T(512)S(1)} %reshape.135, bf16[512,2048]{1,0:T(8,128)(2,1)S(1)} %bitcast.37, bf16[1,512,2048]{2,1,0:T(8,128)(2,1)} %all-gather.3.cloned.1.call-done), kind=kOutput, calls=%fused_computation.20 | convolution fusion | flops 1077673472 | bytes 5770240 | tf_op jit(solution)/shard_map/dot_general | solution.py:18
  145.0 2.6 %fusion = bf16[1,2048,512]{2,1,0:T(8,128)(2,1)} fusion(bf16[512,2048]{1,0:T(8,128)(2,1)S(1)} %bitcast.40, bf16[512,512]{0,1:T(8,128)(2,1)S(1)} %get-tuple-element.16), kind=kOutput, calls=%fused_computation.10 | convolution fusion | flops 1074790400 | bytes 4718592 | tf_op jit(solution)/shard_map/dot_general | solution.py:28
  148.3 3.6 %all-to-all-start.4 = ((bf16[8,64,1]{1,2,0:T(2,128)(2,1)}), bf16[8,64,1]{1,2,0:T(2,128)(2,1)S(1)}, u32[]{:S(2)}, u32[]{:S(2)}) async-start(bf16[8,64,1]{1,2,0:T(2,128)(2,1)} %convert_element_type.100), calls=%async_computation.4 | async-start | bytes 8192 | tf_op jit(solution)/shard_map/all_to_all | solution.py:75
  152.0 2.7 %convolution_convert_fusion.2 = bf16[512,2048]{1,0:T(8,128)(2,1)} fusion(bf16[512,512]{0,1:T(8,128)(2,1)S(1)} %get-tuple-element.16, bf16[1,2048,512]{2,1,0:T(8,128)(2,1)S(1)} %copy-done.5), kind=kOutput, calls=%fused_computation.9 | convolution fusion | flops 1074790400 | bytes 4718592 | tf_op jit(solution)/shard_map/dot_general | solution.py:25
  154.7 3.7 %all-to-all-done.4 = bf16[8,64,1]{1,2,0:T(2,128)(2,1)S(1)} async-done(((bf16[8,64,1]{1,2,0:T(2,128)(2,1)}), bf16[8,64,1]{1,2,0:T(2,128)(2,1)S(1)}, u32[]{:S(2)}, u32[]{:S(2)}) %all-to-all-start.4) | async-done | bytes 1056 | tf_op jit(solution)/shard_map/all_to_all | solution.py:75
  158.4 3.6 %all-to-all-start.3 = ((bf16[8,64,2048]{2,1,0:T(8,128)(2,1)}), bf16[8,64,2048]{2,1,0:T(8,128)(2,1)S(1)}, u32[]{:S(2)}, u32[]{:S(2)}) async-start(bf16[8,64,2048]{2,1,0:T(8,128)(2,1)} %bitcast.41), calls=%async_computation.3 | async-start | bytes 4194304 | tf_op jit(solution)/shard_map/all_to_all | solution.py:74
  162.2 4.7 %fusion.1 = bf16[1,512,2048]{2,1,0:T(8,128)(2,1)} fusion(bf16[512,2048]{1,0:T(8,128)(2,1)} %bitcast.38, f32[512]{0:T(512)S(1)} %reshape.135, f32[512,512]{0,1:T(8,128)} %fusion.3), kind=kOutput, calls=%fused_computation.11 | convolution fusion | flops 1079246848 | bytes 5244928 | tf_op jit(solution)/shard_map/dot_general | solution.py:31
  167.1 1.9 gather_fusion.2
  169.8 39.4 %all-to-all-done.3 = bf16[8,64,2048]{2,1,0:T(8,128)(2,1)S(1)} async-done(((bf16[8,64,2048]{2,1,0:T(8,128)(2,1)}), bf16[8,64,2048]{2,1,0:T(8,128)(2,1)S(1)}, u32[]{:S(2)}, u32[]{:S(2)}) %all-to-all-start.3) | async-done | bytes 2097184 | tf_op jit(solution)/shard_map/all_to_all | solution.py:74
  209.2 2.3 %gather_fusion.1 = bf16[256,2048]{1,0:T(8,128)(2,1)} fusion(bf16[512,2048]{1,0:T(8,128)(2,1)S(1)} %bitcast.35, s32[1024]{0:T(1024)S(1)} %pad_clamp_fusion), kind=kCustom, calls=%fused_computation.3 | custom fusion | bytes 2098176 | tf_op jit(solution)/shard_map/gather | solution.py:79
  211.5 1.8 reshape.133
  213.2 1.5 fusion.15
  214.8 1.4 fusion.8
  216.1 2.1 convert_element_type.93
  218.3 2.1 convert_element_type.98
  (50 shorter events, 5.1 us)
Async XLA Ops:
  7.2 16.7 %copy-start = (bf16[128,2048]{1,0:T(8,128)(2,1)S(1)}, bf16[128,2048]{1,0:T(8,128)(2,1)}, u32[]{:S(2)}) copy-start(bf16[128,2048]{1,0:T(8,128)(2,1)} %param.9) | copy-start | bytes 1572868
  16.6 17.0 %all-to-all-start = ((bf16[8,64,1]{1,2,0:T(2,128)(2,1)}), bf16[8,64,1]{1,2,0:T(2,128)(2,1)S(1)}, u32[]{:S(2)}, u32[]{:S(2)}) async-start(bf16[8,64,1]{1,2,0:T(2,128)(2,1)} %select_n.52), calls=%async_computation | async-start | bytes 8192 | tf_op jit(solution)/shard_map/all_to_all | solution.py:67
  23.9 2.5 %copy-start.1 = (bf16[128,2048]{1,0:T(8,128)(2,1)S(1)}, bf16[128,2048]{1,0:T(8,128)(2,1)}, u32[]{:S(2)}) copy-start(bf16[128,2048]{1,0:T(8,128)(2,1)} %param.8) | copy-start | bytes 1572868
  33.6 53.7 %all-to-all-start.2 = ((bf16[8,64,2048]{2,1,0:T(8,128)(2,1)}), bf16[8,64,2048]{2,1,0:T(8,128)(2,1)S(1)}, u32[]{:S(2)}, u32[]{:S(2)}) async-start(bf16[8,64,2048]{2,1,0:T(8,128)(2,1)} %bitcast.36), calls=%async_computation.2 | async-start | bytes 4194304 | tf_op jit(solution)/shard_map/all_to_all | solution.py:65
  39.6 53.5 %all-gather.5.cloned.1.call-start = ((), (), s32[]{:S(2)}) async-start(), calls=%async_computation.8 | async-start | bytes 2621440 | tf_op jit(solution)/shard_map/all_gather | solution.py:43
  87.3 1.3 copy-start.3
  88.6 52.1 %all-to-all-start.1 = ((bf16[8,64,2048]{2,1,0:T(8,128)(2,1)}), bf16[8,64,2048]{2,1,0:T(8,128)(2,1)S(1)}, u32[]{:S(2)}, u32[]{:S(2)}) async-start(bf16[8,64,2048]{2,1,0:T(8,128)(2,1)} %bitcast.4), calls=%async_computation.1 | async-start | bytes 4194304 | tf_op jit(solution)/shard_map/all_to_all | solution.py:66
  92.2 26.5 %all-gather.3.cloned.1.call-start = ((), (), s32[]{:S(2)}) async-start(), calls=%async_computation.7 | async-start | bytes 2621440 | tf_op jit(solution)/shard_map/all_gather | solution.py:44
  93.0 123.1 %reduce-scatter.3.cloned.1.call-start = ((), (), s32[]{:S(2)}) async-start(), calls=%async_computation.9 | async-start | bytes 2621440 | tf_op jit(solution)/shard_map/reduce_scatter | solution.py:85
  140.7 4.3 %copy-start.2 = (bf16[8,64,2048]{2,1,0:T(8,128)(2,1)}, bf16[8,64,2048]{2,1,0:T(8,128)(2,1)S(1)}, u32[]{:S(2)}) copy-start(bf16[8,64,2048]{2,1,0:T(8,128)(2,1)S(1)} %all-to-all-done.1) | copy-start | bytes 6291460
  140.7 4.3 %copy-start.4 = (bf16[8,64,2048]{2,1,0:T(8,128)(2,1)S(1)}, bf16[8,64,2048]{2,1,0:T(8,128)(2,1)}, u32[]{:S(2)}) copy-start(bf16[8,64,2048]{2,1,0:T(8,128)(2,1)} %copy-done.3) | copy-start | bytes 6291460
  147.6 4.3 %copy-start.5 = (bf16[1,2048,512]{2,1,0:T(8,128)(2,1)S(1)}, bf16[1,2048,512]{2,1,0:T(8,128)(2,1)}, u32[]{:S(2)}) copy-start(bf16[1,2048,512]{2,1,0:T(8,128)(2,1)} %all-gather.5.cloned.1.call-done) | copy-start | bytes 6291460
  148.3 10.0 %all-to-all-start.4 = ((bf16[8,64,1]{1,2,0:T(2,128)(2,1)}), bf16[8,64,1]{1,2,0:T(2,128)(2,1)S(1)}, u32[]{:S(2)}, u32[]{:S(2)}) async-start(bf16[8,64,1]{1,2,0:T(2,128)(2,1)} %convert_element_type.100), calls=%async_computation.4 | async-start | bytes 8192 | tf_op jit(solution)/shard_map/all_to_all | solution.py:75
  158.4 50.8 %all-to-all-start.3 = ((bf16[8,64,2048]{2,1,0:T(8,128)(2,1)}), bf16[8,64,2048]{2,1,0:T(8,128)(2,1)S(1)}, u32[]{:S(2)}, u32[]{:S(2)}) async-start(bf16[8,64,2048]{2,1,0:T(8,128)(2,1)} %bitcast.41), calls=%async_computation.3 | async-start | bytes 4194304 | tf_op jit(solution)/shard_map/all_to_all | solution.py:74
  162.0 56.3 %reduce-scatter.5.cloned.1.call-start = ((), (), s32[]{:S(2)}) async-start(), calls=%async_computation.10 | async-start | bytes 2621440 | tf_op jit(solution)/shard_map/reduce_scatter | solution.py:88
Sparse Core Ops, SparseCore 0:
  42.0 24.0 all-gather.4
  94.7 24.0 all-gather.2
  147.8 30.5 reduce-scatter.2
  180.9 31.4 reduce-scatter.4
where the time goes:
time: 228 us; the launch traced here: 227 us
  waiting for transfers between devices  134 us (59%)
  starting transfers between devices  24.5 us (11%)
  local copies, waits for them, and re-layouts  24.2 us (11%)
  matrix products  18.9 us (8%)
  between operations  14 us (6%)
  other arithmetic  11 us (5%)
    all_to_all x1, waiting for transfers between devices, on_device(): lax.all_to_all(outbound_inputs, 'expert', split_axis=0, concat_axis=0, ti...  46.9 us
    all_to_all x1, waiting for transfers between devices, on_device(): lax.all_to_all(back_rows, 'expert', split_axis=0, concat_axis=0, tiled=True)  39.4 us
    all_to_all x1, waiting for transfers between devices, on_device(): lax.all_to_all(outbound_grads, 'expert', split_axis=0, concat_axis=0, til...  22 us
    all_gather x1, waiting for transfers between devices, on_device(): lax.all_gather(weight_out, 'dp', axis=2, tiled=True)  21.1 us
    all_to_all x1, starting transfers between devices, on_device(): lax.all_to_all(outbound_gates, 'expert', split_axis=0, concat_axis=0, til...  7.25 us
    all_to_all x1, starting transfers between devices, on_device(): lax.all_to_all(outbound_inputs, 'expert', split_axis=0, concat_axis=0, ti...  6 us
    dot_general x1, matrix products, backward_rows(): lax.dot_general(hidden_act, scaled, (((0,), (0,)), ((), ())), preferred_e...  4.74 us
  transfers between devices with their start and end apart: 9, of which 5 were waited for; matrix products, arithmetic and copies ran while one was open for 15% of the time, Pallas kernels for 0%

commit v1 on v0

v1 whole, which is shorter than its diff:
```python
import functools

import jax
import jax.numpy as jnp
from jax import lax
from jax.experimental import pallas as pl
from jax.experimental.pallas import tpu as pltpu
from jax.sharding import PartitionSpec as P

BF16 = jnp.bfloat16
F32 = jnp.float32
VMEM_LIMIT = 50 * 1024 * 1024
TILE = 256


def swap(value, axis, bit):
    return lax.ppermute(value, axis, [(i, i ^ bit) for i in range(lax.axis_size(axis))])


def bits_of(count):
    return [1 << b for b in reversed(range(count.bit_length() - 1))]


def plus(a, b):
    return (a.astype(F32) + b.astype(F32)).astype(BF16)


def wide(a, b):
    return a.astype(F32) + b.astype(F32)


def dot(a, b, ca=1, cb=0):
    return lax.dot_general(a, b, (((ca,), (cb,)), ((), ())), preferred_element_type=F32)


ANY = pl.BlockSpec(memory_space=pl.ANY)
VMEM = pl.BlockSpec(memory_space=pltpu.VMEM)
SMEM = pl.BlockSpec(memory_space=pltpu.SMEM)


def call(body, name, in_specs, out_shape, scratch, flops, moved):
    return pl.pallas_call(
        body,
        name=name,
        in_specs=in_specs,
        out_specs=[VMEM] * len(out_shape),
        out_shape=out_shape,
        scratch_shapes=scratch,
        compiler_params=pltpu.CompilerParams(vmem_limit_bytes=VMEM_LIMIT),
        cost_estimate=pl.CostEstimate(flops=flops, bytes_accessed=moved, transcendentals=0),
    )


def shape(*dims, dtype=BF16):
    return jax.ShapeDtypeStruct(dims, dtype)


class Copies:
    def __init__(self, sems):
        self.sems = sems
        self.count = 0

    def start(self, src, dst):
        copy = pltpu.make_async_copy(src, dst, self.sems.at[self.count])
        self.count += 1
        copy.start()
        return copy


def prepare_body(ids, gates, weight_in, weight_out, table, stack):
    lanes = lax.broadcasted_iota(jnp.int32, table.shape, 1)
    total = jnp.zeros(table.shape, F32)
    for k in range(2):
        total += jnp.where(lanes == ids[:, k : k + 1], gates[:, k : k + 1].astype(F32), 0.0)
    table[...] = total.astype(BF16)
    stack[0] = weight_in[0]
    stack[1] = weight_out[0].T


def start_rows(copies, blocks, dst):
    rows = blocks[0].shape[0]
    return [copies.start(b, dst.at[pl.ds(i * rows, rows)]) for i, b in enumerate(blocks)]


def start_weights(copies, pieces, which, me_d, dst):
    depth = dst.shape[1] // (len(pieces) // 2)
    started = {0: [], 1: []}
    for (s, m), ref in sorted(pieces.items()):
        place = pl.multiple_of((me_d ^ m) * depth, depth)
        started[s].append(copies.start(ref.at[which], dst.at[s, pl.ds(place, depth)]))
    return started


def wait(copies):
    for copy in copies:
        copy.wait()


def forward_body(blocks, keys, share, *refs):
    place, refs = refs[0], refs[1:]
    tok, refs = refs[:blocks], refs[blocks:]
    tables, refs = refs[:blocks], refs[blocks:]
    pieces, refs = dict(zip(keys, refs)), refs[len(keys) :]
    hid, slope_out, act_t, tok_t, t, w, sems = refs
    me_e, me_d = place[0], place[1]
    copies = Copies(sems)
    rows_in = start_rows(copies, tok, t)
    weights_in = start_weights(copies, pieces, 0, me_d, w)
    lanes = lax.broadcasted_iota(jnp.int32, tables[0].shape, 1)

    def gate_of(s):
        e = me_e ^ (share * s)
        columns = [
            jnp.sum(jnp.where(lanes == e, tb[...].astype(F32), 0.0), axis=1, keepdims=True)
            for tb in tables
        ]
        return jnp.concatenate(columns, axis=0)

    gates = [gate_of(s) for s in range(2)]
    wait(rows_in)
    width, hidden = w.shape[1:]

    @pl.loop(0, width // TILE)
    def _(j):
        at = pl.ds(pl.multiple_of(j * TILE, TILE), TILE)
        tok_t[at, :] = t[:, at].T

    for s in range(2):
        wait(weights_in[s])

        @pl.loop(0, hidden // TILE)
        def _(j, s=s):
            at = pl.ds(pl.multiple_of(j * TILE, TILE), TILE)
            to = pl.ds(pl.multiple_of(s * hidden + j * TILE, TILE), TILE)
            preact = dot(t[...], w[s, :, at])
            logistic = jax.nn.sigmoid(preact)
            act = preact * logistic
            hid[:, to] = act.astype(BF16)
            slope_out[:, to] = (gates[s] * (logistic * (1.0 + preact * (1.0 - logistic)))).astype(BF16)
            act_t[to, :] = (gates[s] * act).astype(BF16).T


def backward_body(blocks, keys, share, order, *refs):
    place, refs = refs[0], refs[1:]
    grd, refs = refs[:blocks], refs[blocks:]
    pieces, refs = dict(zip(keys, refs)), refs[len(keys) :]
    hid, slope, tok_t, pre, table, keep, send, g, w, sems = refs
    me_e, me_d = place[0], place[1]
    copies = Copies(sems)
    weights_in = start_weights(copies, pieces, 1, me_d, w)
    rows_in = start_rows(copies, grd, g)
    width, hidden = w.shape[1:]
    rows = g.shape[0]
    depth = keep.shape[1]
    wait(rows_in)
    columns = {}
    for s in (1, 0):
        wait(weights_in[s])

        def step(j, total, s=s):
            at = pl.ds(pl.multiple_of(j * TILE, TILE), TILE)
            to = pl.ds(pl.multiple_of(s * hidden + j * TILE, TILE), TILE)
            back = dot(g[...], w[s, :, at])
            pre[:, to] = (slope[:, to].astype(F32) * back).astype(BF16)
            return total + jnp.sum(hid[:, to].astype(F32) * back, axis=1, keepdims=True)

        columns[s] = lax.fori_loop(0, hidden // TILE, step, jnp.zeros((rows, 1), F32))
        if s:

            @pl.loop(0, width // depth // 2)
            def _(j, s=s):
                for out, core in ((keep, 0), (send, 1)):
                    at = pl.ds(pl.multiple_of((me_d ^ (2 * j + core)) * depth, depth), depth)
                    out[j] = dot(tok_t[at, :], pre[:, s * hidden :]).astype(BF16)

    lanes = lax.broadcasted_iota(jnp.int32, (rows, table.shape[1]), 1)
    total = jnp.zeros(lanes.shape, F32)
    for s in range(2):
        total += jnp.where(lanes == me_e ^ (share * s), columns[s], 0.0)
    table[...] = total.astype(BF16)


def route_body(blocks, keys, first, *refs):
    place, refs = refs[0], refs[1:]
    pieces, refs = dict(zip(keys, refs)), refs[len(keys) :]
    source, refs = refs[0], refs[1:]
    outs, (w, pre, sems) = refs[:blocks], refs[blocks:]
    copies = Copies(sems)
    wait([copies.start(source.at[pl.ds(first, pre.shape[0])], pre)])
    weights_in = start_weights(copies, pieces, 0, place[1], w)
    wait(weights_in[0])
    wait(weights_in[1])
    width, hidden = w.shape[1:]
    rows = outs[0].shape[0]

    @pl.loop(0, width // TILE)
    def _(j):
        at = pl.ds(pl.multiple_of(j * TILE, TILE), TILE)
        total = dot(pre[:, :hidden], w[0, at, :], 1, 1) + dot(pre[:, hidden:], w[1, at, :], 1, 1)
        for i, out in enumerate(outs):
            out[:, at] = total[i * rows : (i + 1) * rows].astype(BF16)


def out_body(blocks, masks, *refs):
    place, refs = refs[0], refs[1:]
    grd, refs = refs[:blocks], refs[blocks:]
    act_t, keep, send, g, sems = refs
    me_d = place[1]
    hidden, depth = keep.shape[2:]
    rows = grd[0].shape[0]
    copies = Copies(sems)
    started = {}
    for n, m in enumerate(masks):
        for core in range(2):
            at = pl.ds(pl.multiple_of((me_d ^ (m | core)) * depth, depth), depth)
            started[n, core] = [
                copies.start(b.at[:, at], g.at[2 * n + core, pl.ds(i * rows, rows)])
                for i, b in enumerate(grd)
            ]
    for n, m in enumerate(masks):
        for core, out in ((1, send), (0, keep)):
            wait(started[n, core])
            for s in range(2):
                out[s, n] = dot(act_t[s * hidden : (s + 1) * hidden, :], g[2 * n + core]).astype(BF16)


def in_body(*refs):
    place, tok_t, pre, keep, send = refs
    me_d = place[1]
    depth = keep.shape[1]

    @pl.loop(0, keep.shape[0])
    def _(j):
        for out, core in ((send, 1), (keep, 0)):
            at = pl.ds(pl.multiple_of((me_d ^ (2 * j + core)) * depth, depth), depth)
            out[j] = dot(tok_t[at, :], pre[:, : keep.shape[2]]).astype(BF16)


def on_device(tokens, out_grad, route_ids, route_gates, weight_in, weight_out):
    local, width = tokens.shape
    experts = lax.axis_size("expert")
    slices = lax.axis_size("dp")
    hidden, depth = weight_in.shape[2], weight_in.shape[1]
    place = jnp.stack([lax.axis_index("expert"), lax.axis_index("dp")]).astype(jnp.int32)

    share = experts // 4
    token_bits = [b for b in bits_of(experts) if b != share]
    dp_bits = bits_of(slices)
    core, others = dp_bits[-1], dp_bits[:-1]

    table, shard = call(
        prepare_body,
        "prepare",
        [VMEM] * 4,
        [shape(local, experts), shape(2, depth, hidden)],
        [],
        0,
        4 * depth * hidden * 2,
    )(route_ids, route_gates, weight_in, weight_out)

    tok, grd, gate = {0: tokens}, {0: out_grad}, {0: table}
    for held in (tok, grd, gate):
        for bit in token_bits:
            for m in list(held):
                held[m | bit] = swap(held[m], "expert", bit)
    order = sorted(tok)
    blocks = len(order)
    rows = blocks * local

    pieces = {(0, 0): shard, (1, 0): swap(shard, "expert", share)}
    for bit in dp_bits:
        for s, m in list(pieces):
            pieces[s, m | bit] = swap(pieces[s, m], "dp", bit)
    keys = sorted(pieces)
    weights = [pieces[k] for k in keys]
    product = 2 * rows * width * hidden

    hid, slope, act_t, tok_t = call(
        functools.partial(forward_body, blocks, keys, share),
        "forward",
        [SMEM] + [ANY] * blocks + [VMEM] * blocks + [ANY] * len(keys),
        [
            shape(rows, 2 * hidden),
            shape(rows, 2 * hidden),
            shape(2 * hidden, rows),
            shape(width, rows),
        ],
        [
            pltpu.VMEM((rows, width), BF16),
            pltpu.VMEM((2, width, hidden), BF16),
            pltpu.SemaphoreType.DMA((blocks + len(keys),)),
        ],
        2 * product,
        4 * rows * width + 4 * width * hidden + 12 * rows * hidden,
    )(place, *[tok[m] for m in order], *[gate[m] for m in order], *weights)

    half = slices // 2
    pre, back_table, in_keep, in_send = call(
        functools.partial(backward_body, blocks, keys, share, order),
        "backward",
        [SMEM] + [ANY] * blocks + [ANY] * len(keys) + [VMEM] * 3,
        [
            shape(rows, 2 * hidden),
            shape(rows, experts),
            shape(half, depth, hidden),
            shape(half, depth, hidden),
        ],
        [
            pltpu.VMEM((rows, width), BF16),
            pltpu.VMEM((2, width, hidden), BF16),
            pltpu.SemaphoreType.DMA((blocks + len(keys),)),
        ],
        3 * product,
        4 * rows * width + 6 * width * hidden + 12 * rows * hidden,
    )(place, *[grd[m] for m in order], *weights, hid, slope, tok_t)

    def route_of(part):
        n = len(part)
        first = order.index(part[0]) * local
        outs = call(
            functools.partial(route_body, n, keys, first),
            "route",
            [SMEM] + [ANY] * (len(keys) + 1),
            [shape(local, width)] * n,
            [
                pltpu.VMEM((2, width, hidden), BF16),
                pltpu.VMEM((n * local, 2 * hidden), BF16),
                pltpu.SemaphoreType.DMA((len(keys) + 1,)),
            ],
            2 * product * n // blocks,
            4 * width * hidden + 2 * n * local * (width + 2 * hidden),
        )(place, *weights, pre)
        return dict(zip(part, outs))

    def out_of(masks):
        n = len(masks)
        return call(
            functools.partial(out_body, blocks, masks),
            "partial_out",
            [SMEM] + [ANY] * blocks + [VMEM],
            [shape(2, n, hidden, depth)] * 2,
            [
                pltpu.VMEM((2 * n, rows, depth), BF16),
                pltpu.SemaphoreType.DMA((2 * n * blocks,)),
            ],
            product,
            3 * rows * width,
        )(place, *[grd[m] for m in order], act_t)

    masks = list(range(0, slices, 2))
    high, low = masks[half // 2 :], masks[: half // 2]

    in_far = plus(in_keep, swap(in_send, "dp", core))
    in_far = swap(in_far, "expert", share)
    keep_high, send_high = out_of(high)
    out_far = plus(keep_high, swap(send_high, "dp", core))
    out_far = swap(out_far, "dp", others[0])

    route = route_of(order[blocks // 2 :])
    route.update(route_of(order[: blocks // 2]))
    home = dict(zip(order, jnp.split(back_table, blocks, axis=0)))
    for bit in reversed(token_bits):
        for m in sorted(route, reverse=True):
            if m & bit:
                route[m ^ bit] = plus(route[m ^ bit], swap(route.pop(m), "expert", bit))
                home[m ^ bit] = plus(home[m ^ bit], swap(home.pop(m), "expert", bit))
    grad_tokens = route[0]
    chosen = route_ids[:, :, None] == jnp.arange(experts, dtype=jnp.int32)
    grad_gates = jnp.sum(jnp.where(chosen, home[0].astype(F32)[:, None, :], 0.0), axis=2)

    keep_low, send_low = out_of(low)
    out_sum = plus(keep_low, swap(send_low, "dp", core))
    out_sum = plus(out_sum, out_far)
    for bit in others[1:]:
        n = out_sum.shape[1] // 2
        out_sum = plus(out_sum[:, :n], swap(out_sum[:, n:], "dp", bit))
    grad_out = wide(out_sum[0, 0], swap(out_sum[1, 0], "expert", share))

    in_keep, in_send = call(
        in_body,
        "partial_in",
        [SMEM, VMEM, VMEM],
        [shape(half, depth, hidden)] * 2,
        [],
        product,
        3 * rows * width,
    )(place, tok_t, pre)
    in_sum = plus(in_keep, swap(in_send, "dp", core))
    in_sum = plus(in_sum, in_far)
    for bit in others:
        n = in_sum.shape[0] // 2
        total = wide if bit == others[-1] else plus
        in_sum = total(in_sum[:n], swap(in_sum[n:], "dp", bit))
    return (grad_tokens, grad_gates.astype(BF16), in_sum, grad_out[None])


def solution(mesh):
    return jax.shard_map(
        on_device,
        mesh=mesh,
        in_specs=(
            P(("dp", "expert"), None),
            P(("dp", "expert"), None),
            P(("dp", "expert"), None),
            P(("dp", "expert"), None),
            P("expert", "dp", None),
            P("expert", None, "dp"),
        ),
        out_specs=(
            P(("dp", "expert"), None),
            P(("dp", "expert"), None),
            P("expert", "dp", None),
            P("expert", None, "dp"),
        ),
        check_vma=False,
    )
```

time: 228 us -> 230 us (level)
  Pallas kernels: 0 us -> 43.6 us
  matrix products: 18.9 us -> 0 us
  between operations: 14 us -> 0.95 us
  local copies, waits for them, and re-layouts: 24.2 us -> 13.9 us
  starting transfers between devices: 24.5 us -> 27.5 us
  waiting for transfers between devices: 134 us -> 131 us
    ppermute x0 -> x30, waiting for transfers between devices: none -> 131 us  [swap(): lax.ppermute(value, axis, [(i, i ^ bit) for i in range(lax.axis_size(axis...]
    all_to_all x5 -> x0, waiting for transfers between devices: 112 us -> none  [the longest x1 46.9 us: on_device(): lax.all_to_all(outbound_inputs, 'expert', split_axis=0, concat_axis=0, ti...]
    pallas_call x0 -> x8, Pallas kernels: none -> 43.6 us  [the longest x2 13.3 us: route_of(): call(functools.partial(route_body, n, keys, first), 'route', [SMEM] + [AN...]
    ppermute x0 -> x30, starting transfers between devices: none -> 27.5 us  [swap(): lax.ppermute(value, axis, [(i, i ^ bit) for i in range(lax.axis_size(axis...]
    all_to_all x5 -> x0, starting transfers between devices: 24.1 us -> none  [the longest x1 7.25 us: on_device(): lax.all_to_all(outbound_gates, 'expert', split_axis=0, concat_axis=0, til...]
    all_gather x2 -> x0, waiting for transfers between devices: 21.1 us -> none  [the longest x1 21.1 us: on_device(): lax.all_gather(weight_out, 'dp', axis=2, tiled=True)]
    dot_general x5 -> x0, matrix products: 18.9 us -> none  [the longest x1 4.74 us: backward_rows(): lax.dot_general(hidden_act, scaled, (((0,), (0,)), ((), ())), preferred_e...]
    gather x5 -> x0, local copies, waits for them, and re-layouts: 13.4 us -> none  [the longest x1 3.36 us: on_device(): jnp.take(route_gates.reshape(-1), route_of_slot, axis=0, mode='fill', fil...]
  transfers between devices with their start and end apart: 9 -> 30, of which waited for: 5 -> 10; matrix products, arithmetic and copies ran while one was open for 15% -> 5% of each run, Pallas kernels for 0% -> 15%
where the time goes in v1:
time: 230 us; the launch traced here: 229 us
  waiting for transfers between devices  131 us (57%)
  Pallas kernels  43.6 us (19%)
  starting transfers between devices  27.5 us (12%)
  local copies, waits for them, and re-layouts  13.9 us (6%)
  other arithmetic  11.6 us (5%)
    ppermute x30, waiting for transfers between devices, swap(): lax.ppermute(value, axis, [(i, i ^ bit) for i in range(lax.axis_size(axis...  131 us
    ppermute x30, starting transfers between devices, swap(): lax.ppermute(value, axis, [(i, i ^ bit) for i in range(lax.axis_size(axis...  27.5 us
    unnamed x52, local copies, waits for them, and re-layouts  13.8 us
    pallas_call x2, Pallas kernels, route_of(): call(functools.partial(route_body, n, keys, first), 'route', [SMEM] + [AN...  13.3 us
    pallas_call x1, Pallas kernels, on_device(): call(functools.partial(backward_body, blocks, keys, share, order), 'backw...  9.89 us
    convert_element_type x7, other arithmetic, plus(): return (a.astype(F32) + b.astype(F32)).astype(BF16)  8.75 us
    pallas_call x2, Pallas kernels, out_of(): call(functools.partial(out_body, blocks, masks), 'partial_out', [SMEM] +...  8.61 us
    pallas_call x1, Pallas kernels, on_device(): call(functools.partial(forward_body, blocks, keys, share), 'forward', [SM...  7.72 us
  transfers between devices with their start and end apart: 30, of which 10 were waited for; matrix products, arithmetic and copies ran while one was open for 5% of the time, Pallas kernels for 15%

profile of v1, /device:TPU:0, one launch (start us, length us, event | category | flops | bytes accessed | tf_op | source)
XLA Modules:
  0.0 229.0 jit_solution(2723072799495568186)
XLA Ops:
  4.6 3.1 %collective-permute-start.3 = (bf16[2,512,512]{2,1,0:T(8,128)(2,1)S(1)}, bf16[2,512,512]{2,1,0:T(8,128)(2,1)}, u32[]{:S(2)}, u32[]{:S(2)}) collective-permute-start(bf16[2,512,512]{2,1,0:T(8,128)(2,1)S(1)} %get-tuple-element.24.refs_9_.refs_5_.refs_1_), channel_id=1, source_target_pairs={{0,2},{1,3},{2,0},{3,1},{4,6},{5,7},{6,4},{7,5},{8,10},{9,11},{10,... | collective-permute-start | bytes 3145736 | tf_op jit(solution)/shard_map/ppermute | solution.py:17
  7.6 1.5 collective-permute-start.1
  9.2 21.7 %collective-permute-done.3.refs_13_.refs_9_.refs_5_ = bf16[2,512,512]{2,1,0:T(8,128)(2,1)} collective-permute-done((bf16[2,512,512]{2,1,0:T(8,128)(2,1)S(1)}, bf16[2,512,512]{2,1,0:T(8,128)(2,1)}, u32[]{:S(2)}, u32[]{:S(2)}) %collective-permute-start.3) | collective-permute-done | bytes 1048608 | tf_op jit(solution)/shard_map/ppermute | solution.py:17
  30.9 1.7 collective-permute-start.5
  32.6 1.5 collective-permute-start.10
  34.1 2.6 %collective-permute-start.11 = (bf16[128,2048]{1,0:T(8,128)(2,1)}, bf16[128,2048]{1,0:T(8,128)(2,1)S(1)}, u32[]{:S(2)}, u32[]{:S(2)}) collective-permute-start(bf16[128,2048]{1,0:T(8,128)(2,1)} %refs_1_.4), channel_id=1, source_target_pairs={{0,4},{1,5},{2,6},{3,7},{4,0},{5,1},{6,2},{7,3},{8,12},{9,13},{10,... | collective-permute-start | bytes 1572872 | tf_op jit(solution)/shard_map/ppermute | solution.py:17
  37.0 23.1 %collective-permute-done.14.refs_7_ = bf16[128,8]{1,0:T(8,128)(2,1)S(1)} collective-permute-done((bf16[128,8]{1,0:T(8,128)(2,1)S(1)}, bf16[128,8]{1,0:T(8,128)(2,1)S(1)}, u32[]{:S(2)}, u32[]{:S(2)}) %collective-permute-start.14) | collective-permute-done | bytes 2080 | tf_op jit(solution)/shard_map/ppermute | solution.py:17
  60.6 3.4 %collective-permute-done.13.refs_6_ = bf16[128,8]{1,0:T(8,128)(2,1)S(1)} collective-permute-done((bf16[128,8]{1,0:T(8,128)(2,1)S(1)}, bf16[128,8]{1,0:T(8,128)(2,1)S(1)}, u32[]{:S(2)}, u32[]{:S(2)}) %collective-permute-start.13) | collective-permute-done | bytes 2080 | tf_op jit(solution)/shard_map/ppermute | solution.py:17
  64.5 3.4 %collective-permute-done.15.refs_8_ = bf16[128,8]{1,0:T(8,128)(2,1)S(1)} collective-permute-done((bf16[128,8]{1,0:T(8,128)(2,1)S(1)}, bf16[128,8]{1,0:T(8,128)(2,1)S(1)}, u32[]{:S(2)}, u32[]{:S(2)}) %collective-permute-start.15) | collective-permute-done | bytes 2080 | tf_op jit(solution)/shard_map/ppermute | solution.py:17
  69.8 21.0 %collective-permute-done.8.refs_3_ = bf16[128,2048]{1,0:T(8,128)(2,1)S(1)} collective-permute-done((bf16[128,2048]{1,0:T(8,128)(2,1)}, bf16[128,2048]{1,0:T(8,128)(2,1)S(1)}, u32[]{:S(2)}, u32[]{:S(2)}) %collective-permute-start.8) | collective-permute-done | bytes 524320 | tf_op jit(solution)/shard_map/ppermute | solution.py:17
  92.1 10.5 %collective-permute-done.12.refs_4_ = bf16[128,2048]{1,0:T(8,128)(2,1)S(1)} collective-permute-done((bf16[128,2048]{1,0:T(8,128)(2,1)S(1)}, bf16[128,2048]{1,0:T(8,128)(2,1)S(1)}, u32[]{:S(2)}, u32[]{:S(2)}) %collective-permute-start.12) | collective-permute-done | bytes 524320 | tf_op jit(solution)/shard_map/ppermute | solution.py:17
  103.9 1.5 collective-permute-start.9
  109.8 7.7 %forward.1 = (bf16[512,1024]{1,0:T(8,128)(2,1)S(1)}, bf16[512,1024]{1,0:T(8,128)(2,1)}, bf16[1024,512]{1,0:T(8,128)(2,1)}, bf16[2048,512]{1,0:T(8,128)(2,1)}) custom-call(s32[2]{0:T(128)S(1)} %pad_add_fusion.refs_0_, bf16[128,2048]{1,0:T(8,128)(2,1)S(1)} %copy-done.14, bf16[128,2048]{1,0:T(8,128)(2,1)S(1)} %copy-done.16, bf16[128,2048]{1,0:T(8,128)(2,1)S(1)} %copy-done.18, ...), custom_call_target="tpu_custom_call" | custom-call | flops 2147483648 | bytes 11534336 | tf_op jit(solution)/shard_map/forward/pallas_call | solution.py:278
  118.5 7.4 %collective-permute-done.9.refs_4_ = bf16[128,2048]{1,0:T(8,128)(2,1)} collective-permute-done((bf16[128,2048]{1,0:T(8,128)(2,1)S(1)}, bf16[128,2048]{1,0:T(8,128)(2,1)}, u32[]{:S(2)}, u32[]{:S(2)}) %collective-permute-start.9) | collective-permute-done | bytes 524320 | tf_op jit(solution)/shard_map/ppermute | solution.py:17
  125.9 9.9 %backward.1 = (bf16[512,1024]{1,0:T(8,128)(2,1)S(1)}, bf16[512,8]{1,0:T(8,128)(2,1)S(1)}, bf16[2,512,512]{2,1,0:T(8,128)(2,1)}, bf16[2,512,512]{2,1,0:T(8,128)(2,1)}) custom-call(s32[2]{0:T(128)S(1)} %pad_add_fusion.refs_0_, bf16[128,2048]{1,0:T(8,128)(2,1)S(1)} %copy-done.7, bf16[128,2048]{1,0:T(8,128)(2,1)S(1)} %collective-permute-done.7.refs_2_, ...), custom_call_target="tpu_custom_call" | custom-call | flops 3221225472 | bytes 13631488 | tf_op jit(solution)/shard_map/backward/pallas_call | solution.py:298
  136.8 4.3 %partial_out.3 = (bf16[2,1,512,512]{3,2,1,0:T(8,128)(2,1)S(1)}, bf16[2,1,512,512]{3,2,1,0:T(8,128)(2,1)}) custom-call(s32[2]{0:T(128)S(1)} %pad_add_fusion.refs_0_, bf16[128,2048]{1,0:T(8,128)(2,1)S(1)} %copy-done.7, bf16[128,2048]{1,0:T(8,128)(2,1)S(1)} %collective-permute-done.7.refs_2_, bf16[128,2048]{1,0:T(8,128)(2,1)S(1)} %collective-permute-done.8.refs_3_, ...), custom_call_target="tpu_custom_call" | custom-call | flops 1073741824 | bytes 3145728 | tf_op jit(solution)/shard_map/partial_out/pallas_call | solution.py:337
  142.0 1.5 collective-permute-start.20
  143.5 7.0 %route.3 = (bf16[128,2048]{1,0:T(8,128)(2,1)S(1)}, bf16[128,2048]{1,0:T(8,128)(2,1)}) custom-call(s32[2]{0:T(128)S(1)} %pad_add_fusion.refs_0_, bf16[2,512,512]{2,1,0:T(8,128)(2,1)S(1)} %copy-done.1, bf16[2,512,512]{2,1,0:T(8,128)(2,1)S(1)} %copy-done.3, bf16[2,512,512]{2,1,0:T(8,128)(2,1)} %collective-permute-done.1.refs_11_.refs_7_.refs_3_, ...), custom_call_target="tpu_custom_call" | custom-call | flops 1073741824 | bytes 5767168 | tf_op jit(solution)/shard_map/route/pallas_call | solution.py:320
  151.9 3.9 %partial_in.1 = (bf16[2,512,512]{2,1,0:T(8,128)(2,1)S(1)}, bf16[2,512,512]{2,1,0:T(8,128)(2,1)}) custom-call(s32[2]{0:T(128)S(1)} %pad_add_fusion.refs_0_, bf16[2048,512]{1,0:T(8,128)(2,1)} %get-tuple-element.28.refs_15_.refs_1_, bf16[512,1024]{1,0:T(8,128)(2,1)S(1)} %copy-done.5), custom_call_target="tpu_custom_call" | custom-call | flops 1073741824 | bytes 3145728 | tf_op jit(solution)/shard_map/partial_in/pallas_call | solution.py:379
  155.8 6.3 %route.2 = (bf16[128,2048]{1,0:T(8,128)(2,1)S(1)}, bf16[128,2048]{1,0:T(8,128)(2,1)S(1)}) custom-call(s32[2]{0:T(128)S(1)} %pad_add_fusion.refs_0_, bf16[2,512,512]{2,1,0:T(8,128)(2,1)S(1)} %copy-done.1, bf16[2,512,512]{2,1,0:T(8,128)(2,1)S(1)} %copy-done.3, bf16[2,512,512]{2,1,0:T(8,128)(2,1)} %collective-permute-done.1.refs_11_.refs_7_.refs_3_, ...), custom_call_target="tpu_custom_call" | custom-call | flops 1073741824 | bytes 5767168 | tf_op jit(solution)/shard_map/route/pallas_call | solution.py:320
  162.8 4.3 %partial_out.2 = (bf16[2,1,512,512]{3,2,1,0:T(8,128)(2,1)S(1)}, bf16[2,1,512,512]{3,2,1,0:T(8,128)(2,1)}) custom-call(s32[2]{0:T(128)S(1)} %pad_add_fusion.refs_0_, bf16[128,2048]{1,0:T(8,128)(2,1)S(1)} %copy-done.7, bf16[128,2048]{1,0:T(8,128)(2,1)S(1)} %collective-permute-done.7.refs_2_, bf16[128,2048]{1,0:T(8,128)(2,1)S(1)} %collective-permute-done.8.refs_3_, ...), custom_call_target="tpu_custom_call" | custom-call | flops 1073741824 | bytes 3145728 | tf_op jit(solution)/shard_map/partial_out/pallas_call | solution.py:337
  167.4 1.3 add_convert_fusion.4
  168.7 5.8 %collective-permute-start.24 = (bf16[2,512,512]{2,1,0:T(8,128)(2,1)}, bf16[2,512,512]{2,1,0:T(8,128)(2,1)}, u32[]{:S(2)}, u32[]{:S(2)}) collective-permute-start(bf16[2,512,512]{2,1,0:T(8,128)(2,1)} %add_convert_fusion.4), channel_id=1, source_target_pairs={{0,2},{1,3},{2,0},{3,1},{4,6},{5,7},{6,4},{7,5},{8,10},{9,11},{10,... | collective-permute-start | bytes 3145736 | tf_op jit(solution)/shard_map/ppermute | solution.py:17
  174.5 1.3 add_convert_fusion.1
  177.3 1.2 collective-permute-start.16
  178.5 1.2 add_convert_fusion.7
  179.9 29.7 %collective-permute-done.24 = bf16[2,512,512]{2,1,0:T(8,128)(2,1)} collective-permute-done((bf16[2,512,512]{2,1,0:T(8,128)(2,1)}, bf16[2,512,512]{2,1,0:T(8,128)(2,1)}, u32[]{:S(2)}, u32[]{:S(2)}) %collective-permute-start.24) | collective-permute-done | bytes 1048608 | tf_op jit(solution)/shard_map/ppermute | solution.py:17
  209.6 2.0 add_convert_fusion.3
  212.5 2.0 add_convert_fusion
  215.7 9.5 %collective-permute-done.25 = bf16[1,512,512]{2,1,0:T(8,128)(2,1)S(1)} collective-permute-done((bf16[1,512,512]{2,1,0:T(8,128)(2,1)S(1)}, bf16[1,512,512]{2,1,0:T(8,128)(2,1)S(1)}, u32[]{:S(2)}, u32[]{:S(2)}) %collective-permute-start.25) | collective-permute-done | bytes 524320 | tf_op jit(solution)/shard_map/ppermute | solution.py:17
  225.2 1.1 convert_add_fusion.1
  226.3 1.5 collective-permute-done.29
  (104 shorter events, 24.2 us)
Async XLA Ops:
  4.5 101.0 %copy-start = (bf16[2,512,512]{2,1,0:T(8,128)(2,1)}, bf16[2,512,512]{2,1,0:T(8,128)(2,1)S(1)}, u32[]{:S(2)}) copy-start(bf16[2,512,512]{2,1,0:T(8,128)(2,1)S(1)} %get-tuple-element.24.refs_9_.refs_5_.refs_1_) | copy-start | bytes 3145732
  4.6 26.4 %collective-permute-start.3 = (bf16[2,512,512]{2,1,0:T(8,128)(2,1)S(1)}, bf16[2,512,512]{2,1,0:T(8,128)(2,1)}, u32[]{:S(2)}, u32[]{:S(2)}) collective-permute-start(bf16[2,512,512]{2,1,0:T(8,128)(2,1)S(1)} %get-tuple-element.24.refs_9_.refs_5_.refs_1_), channel_id=1, source_target_pairs={{0,2},{1,3},{2,0},{3,1},{4,6},{5,7},{6,4},{7,5},{8,10},{9,11},{10,... | collective-permute-start | bytes 3145736 | tf_op jit(solution)/shard_map/ppermute | solution.py:17
  7.6 61.6 %collective-permute-start.1 = (bf16[2,512,512]{2,1,0:T(8,128)(2,1)S(1)}, bf16[2,512,512]{2,1,0:T(8,128)(2,1)}, u32[]{:S(2)}, u32[]{:S(2)}) collective-permute-start(bf16[2,512,512]{2,1,0:T(8,128)(2,1)S(1)} %get-tuple-element.24.refs_9_.refs_5_.refs_1_), channel_id=1, source_target_pairs={{0,16},{8,24},{16,0},{24,8},{1,17},{9,25},{17,1},{25,9},{2,18},{10... | collective-permute-start | bytes 3145736 | tf_op jit(solution)/shard_map/ppermute | solution.py:17
  30.9 38.4 %collective-permute-start.5 = (bf16[2,512,512]{2,1,0:T(8,128)(2,1)}, bf16[2,512,512]{2,1,0:T(8,128)(2,1)}, u32[]{:S(2)}, u32[]{:S(2)}) collective-permute-start(bf16[2,512,512]{2,1,0:T(8,128)(2,1)} %collective-permute-done.3.refs_13_.refs_9_.refs_5_), channel_id=1, source_target_pairs={{0,16},{8,24},{16,0},{24,8},{1,17},{9,25},{17,1},{25,9},{2,18},{10... | collective-permute-start | bytes 3145736 | tf_op jit(solution)/shard_map/ppermute | solution.py:17
  32.6 35.3 %collective-permute-start.10 = (bf16[128,2048]{1,0:T(8,128)(2,1)}, bf16[128,2048]{1,0:T(8,128)(2,1)S(1)}, u32[]{:S(2)}, u32[]{:S(2)}) collective-permute-start(bf16[128,2048]{1,0:T(8,128)(2,1)} %refs_1_.4), channel_id=1, source_target_pairs={{0,1},{1,0},{2,3},{3,2},{4,5},{5,4},{6,7},{7,6},{8,9},{9,8},{10,11... | collective-permute-start | bytes 1572872 | tf_op jit(solution)/shard_map/ppermute | solution.py:17
  34.1 34.6 %collective-permute-start.11 = (bf16[128,2048]{1,0:T(8,128)(2,1)}, bf16[128,2048]{1,0:T(8,128)(2,1)S(1)}, u32[]{:S(2)}, u32[]{:S(2)}) collective-permute-start(bf16[128,2048]{1,0:T(8,128)(2,1)} %refs_1_.4), channel_id=1, source_target_pairs={{0,4},{1,5},{2,6},{3,7},{4,0},{5,1},{6,2},{7,3},{8,12},{9,13},{10,... | collective-permute-start | bytes 1572872 | tf_op jit(solution)/shard_map/ppermute | solution.py:17
  36.7 23.4 %collective-permute-start.14 = (bf16[128,8]{1,0:T(8,128)(2,1)S(1)}, bf16[128,8]{1,0:T(8,128)(2,1)S(1)}, u32[]{:S(2)}, u32[]{:S(2)}) collective-permute-start(bf16[128,8]{1,0:T(8,128)(2,1)S(1)} %get-tuple-element.25.refs_5_), channel_id=1, source_target_pairs={{0,4},{1,5},{2,6},{3,7},{4,0},{5,1},{6,2},{7,3},{8,12},{9,13},{10,... | collective-permute-start | bytes 6152 | tf_op jit(solution)/shard_map/ppermute | solution.py:17
  60.1 3.9 %collective-permute-start.13 = (bf16[128,8]{1,0:T(8,128)(2,1)S(1)}, bf16[128,8]{1,0:T(8,128)(2,1)S(1)}, u32[]{:S(2)}, u32[]{:S(2)}) collective-permute-start(bf16[128,8]{1,0:T(8,128)(2,1)S(1)} %get-tuple-element.25.refs_5_), channel_id=1, source_target_pairs={{0,1},{1,0},{2,3},{3,2},{4,5},{5,4},{6,7},{7,6},{8,9},{9,8},{10,11... | collective-permute-start | bytes 6152 | tf_op jit(solution)/shard_map/ppermute | solution.py:17
  64.0 3.9 %collective-permute-start.15 = (bf16[128,8]{1,0:T(8,128)(2,1)S(1)}, bf16[128,8]{1,0:T(8,128)(2,1)S(1)}, u32[]{:S(2)}, u32[]{:S(2)}) collective-permute-start(bf16[128,8]{1,0:T(8,128)(2,1)S(1)} %collective-permute-done.14.refs_7_), channel_id=1, source_target_pairs={{0,1},{1,0},{2,3},{3,2},{4,5},{5,4},{6,7},{7,6},{8,9},{9,8},{10,11... | collective-permute-start | bytes 6152 | tf_op jit(solution)/shard_map/ppermute | solution.py:17
  67.9 22.8 %collective-permute-start.8 = (bf16[128,2048]{1,0:T(8,128)(2,1)}, bf16[128,2048]{1,0:T(8,128)(2,1)S(1)}, u32[]{:S(2)}, u32[]{:S(2)}) collective-permute-start(bf16[128,2048]{1,0:T(8,128)(2,1)} %refs_1_.7), channel_id=1, source_target_pairs={{0,4},{1,5},{2,6},{3,7},{4,0},{5,1},{6,2},{7,3},{8,12},{9,13},{10,... | collective-permute-start | bytes 1572872 | tf_op jit(solution)/shard_map/ppermute | solution.py:17
  68.7 35.2 %collective-permute-start = (bf16[2,512,512]{2,1,0:T(8,128)(2,1)S(1)}, bf16[2,512,512]{2,1,0:T(8,128)(2,1)S(1)}, u32[]{:S(2)}, u32[]{:S(2)}) collective-permute-start(bf16[2,512,512]{2,1,0:T(8,128)(2,1)S(1)} %get-tuple-element.24.refs_9_.refs_5_.refs_1_), channel_id=1, source_target_pairs={{0,8},{8,0},{16,24},{24,16},{1,9},{9,1},{17,25},{25,17},{2,10},{10... | collective-permute-start | bytes 3145736 | tf_op jit(solution)/shard_map/ppermute | solution.py:17
  68.7 36.8 %collective-permute-start.4 = (bf16[2,512,512]{2,1,0:T(8,128)(2,1)}, bf16[2,512,512]{2,1,0:T(8,128)(2,1)}, u32[]{:S(2)}, u32[]{:S(2)}) collective-permute-start(bf16[2,512,512]{2,1,0:T(8,128)(2,1)} %collective-permute-done.3.refs_13_.refs_9_.refs_5_), channel_id=1, source_target_pairs={{0,8},{8,0},{16,24},{24,16},{1,9},{9,1},{17,25},{25,17},{2,10},{10... | collective-permute-start | bytes 3145736 | tf_op jit(solution)/shard_map/ppermute | solution.py:17
  69.2 36.3 %collective-permute-start.2 = (bf16[2,512,512]{2,1,0:T(8,128)(2,1)}, bf16[2,512,512]{2,1,0:T(8,128)(2,1)}, u32[]{:S(2)}, u32[]{:S(2)}) collective-permute-start(bf16[2,512,512]{2,1,0:T(8,128)(2,1)} %collective-permute-done.1.refs_11_.refs_7_.refs_3_), channel_id=1, source_target_pairs={{0,8},{8,0},{16,24},{24,16},{1,9},{9,1},{17,25},{25,17},{2,10},{10... | collective-permute-start | bytes 3145736 | tf_op jit(solution)/shard_map/ppermute | solution.py:17
  69.3 36.2 %collective-permute-start.6 = (bf16[2,512,512]{2,1,0:T(8,128)(2,1)}, bf16[2,512,512]{2,1,0:T(8,128)(2,1)}, u32[]{:S(2)}, u32[]{:S(2)}) collective-permute-start(bf16[2,512,512]{2,1,0:T(8,128)(2,1)} %collective-permute-done.5.refs_15_.refs_11_.refs_7_), channel_id=1, source_target_pairs={{0,8},{8,0},{16,24},{24,16},{1,9},{9,1},{17,25},{25,17},{2,10},{10... | collective-permute-start | bytes 3145736 | tf_op jit(solution)/shard_map/ppermute | solution.py:17
  90.7 11.9 %collective-permute-start.12 = (bf16[128,2048]{1,0:T(8,128)(2,1)S(1)}, bf16[128,2048]{1,0:T(8,128)(2,1)S(1)}, u32[]{:S(2)}, u32[]{:S(2)}) collective-permute-start(bf16[128,2048]{1,0:T(8,128)(2,1)S(1)} %collective-permute-done.11.refs_3_), channel_id=1, source_target_pairs={{0,1},{1,0},{2,3},{3,2},{4,5},{5,4},{6,7},{7,6},{8,9},{9,8},{10,11... | collective-permute-start | bytes 1572872 | tf_op jit(solution)/shard_map/ppermute | solution.py:17
  103.4 15.1 %collective-permute-start.7 = (bf16[128,2048]{1,0:T(8,128)(2,1)}, bf16[128,2048]{1,0:T(8,128)(2,1)S(1)}, u32[]{:S(2)}, u32[]{:S(2)}) collective-permute-start(bf16[128,2048]{1,0:T(8,128)(2,1)} %refs_1_.7), channel_id=1, source_target_pairs={{0,1},{1,0},{2,3},{3,2},{4,5},{5,4},{6,7},{7,6},{8,9},{9,8},{10,11... | collective-permute-start | bytes 1572872 | tf_op jit(solution)/shard_map/ppermute | solution.py:17
  103.9 22.0 %collective-permute-start.9 = (bf16[128,2048]{1,0:T(8,128)(2,1)S(1)}, bf16[128,2048]{1,0:T(8,128)(2,1)}, u32[]{:S(2)}, u32[]{:S(2)}) collective-permute-start(bf16[128,2048]{1,0:T(8,128)(2,1)S(1)} %collective-permute-done.8.refs_3_), channel_id=1, source_target_pairs={{0,1},{1,0},{2,3},{3,2},{4,5},{5,4},{6,7},{7,6},{8,9},{9,8},{10,11... | collective-permute-start | bytes 1572872 | tf_op jit(solution)/shard_map/ppermute | solution.py:17
  105.5 20.4 %copy-start.7 = (bf16[128,2048]{1,0:T(8,128)(2,1)S(1)}, bf16[128,2048]{1,0:T(8,128)(2,1)}, u32[]{:S(2)}) copy-start(bf16[128,2048]{1,0:T(8,128)(2,1)} %refs_1_.7) | copy-start | bytes 1572868
  136.8 30.5 %collective-permute-start.23 = (bf16[2,512,512]{2,1,0:T(8,128)(2,1)}, bf16[2,512,512]{2,1,0:T(8,128)(2,1)S(1)}, u32[]{:S(2)}, u32[]{:S(2)}) collective-permute-start(bf16[2,512,512]{2,1,0:T(8,128)(2,1)} %get-tuple-element.38), channel_id=1, source_target_pairs={{0,8},{8,0},{16,24},{24,16},{1,9},{9,1},{17,25},{25,17},{2,10},{10... | collective-permute-start | bytes 3145736 | tf_op jit(solution)/shard_map/ppermute | solution.py:17
  141.1 27.6 %collective-permute-start.27 = (bf16[2,1,512,512]{3,2,1,0:T(8,128)(2,1)}, bf16[2,1,512,512]{3,2,1,0:T(8,128)(2,1)S(1)}, u32[]{:S(2)}, u32[]{:S(2)}) collective-permute-start(bf16[2,1,512,512]{3,2,1,0:T(8,128)(2,1)} %get-tuple-element.43), channel_id=1, source_target_pairs={{0,8},{8,0},{16,24},{24,16},{1,9},{9,1},{17,25},{25,17},{2,10},{10... | collective-permute-start | bytes 3145736 | tf_op jit(solution)/shard_map/ppermute | solution.py:17
  141.5 34.3 %collective-permute-start.19 = (bf16[128,8]{1,0:T(8,128)(2,1)S(1)}, bf16[128,8]{1,0:T(8,128)(2,1)S(1)}, u32[]{:S(2)}, u32[]{:S(2)}) collective-permute-start(bf16[128,8]{1,0:T(8,128)(2,1)S(1)} %get-tuple-element.44), channel_id=1, source_target_pairs={{0,1},{1,0},{2,3},{3,2},{4,5},{5,4},{6,7},{7,6},{8,9},{9,8},{10,11... | collective-permute-start | bytes 6152 | tf_op jit(solution)/shard_map/ppermute | solution.py:17
  142.0 25.2 %collective-permute-start.20 = (bf16[128,8]{1,0:T(8,128)(2,1)S(1)}, bf16[128,8]{1,0:T(8,128)(2,1)S(1)}, u32[]{:S(2)}, u32[]{:S(2)}) collective-permute-start(bf16[128,8]{1,0:T(8,128)(2,1)S(1)} %get-tuple-element.45), channel_id=1, source_target_pairs={{0,1},{1,0},{2,3},{3,2},{4,5},{5,4},{6,7},{7,6},{8,9},{9,8},{10,11... | collective-permute-start | bytes 6152 | tf_op jit(solution)/shard_map/ppermute | solution.py:17
  151.4 25.9 %collective-permute-start.17 = (bf16[128,2048]{1,0:T(8,128)(2,1)}, bf16[128,2048]{1,0:T(8,128)(2,1)}, u32[]{:S(2)}, u32[]{:S(2)}) collective-permute-start(bf16[128,2048]{1,0:T(8,128)(2,1)} %get-tuple-element.33), channel_id=1, source_target_pairs={{0,1},{1,0},{2,3},{3,2},{4,5},{5,4},{6,7},{7,6},{8,9},{9,8},{10,11... | collective-permute-start | bytes 1572872 | tf_op jit(solution)/shard_map/ppermute | solution.py:17
  167.2 12.5 %collective-permute-start.22 = (bf16[2,512,512]{2,1,0:T(8,128)(2,1)}, bf16[2,512,512]{2,1,0:T(8,128)(2,1)}, u32[]{:S(2)}, u32[]{:S(2)}) collective-permute-start(bf16[2,512,512]{2,1,0:T(8,128)(2,1)} %get-tuple-element.36), channel_id=1, source_target_pairs={{0,8},{8,0},{16,24},{24,16},{1,9},{9,1},{17,25},{25,17},{2,10},{10... | collective-permute-start | bytes 3145736 | tf_op jit(solution)/shard_map/ppermute | solution.py:17
  167.3 8.5 %collective-permute-start.21 = (bf16[128,8]{1,0:T(8,128)(2,1)S(1)}, bf16[128,8]{1,0:T(8,128)(2,1)S(1)}, u32[]{:S(2)}, u32[]{:S(2)}) collective-permute-start(bf16[128,8]{1,0:T(8,128)(2,1)S(1)} %add_convert_fusion.10), channel_id=1, source_target_pairs={{0,4},{1,5},{2,6},{3,7},{4,0},{5,1},{6,2},{7,3},{8,12},{9,13},{10,... | collective-permute-start | bytes 6152 | tf_op jit(solution)/shard_map/ppermute | solution.py:17
  168.7 40.9 %collective-permute-start.24 = (bf16[2,512,512]{2,1,0:T(8,128)(2,1)}, bf16[2,512,512]{2,1,0:T(8,128)(2,1)}, u32[]{:S(2)}, u32[]{:S(2)}) collective-permute-start(bf16[2,512,512]{2,1,0:T(8,128)(2,1)} %add_convert_fusion.4), channel_id=1, source_target_pairs={{0,2},{1,3},{2,0},{3,1},{4,6},{5,7},{6,4},{7,5},{8,10},{9,11},{10,... | collective-permute-start | bytes 3145736 | tf_op jit(solution)/shard_map/ppermute | solution.py:17
  175.8 36.7 %collective-permute-start.26 = (bf16[2,1,512,512]{3,2,1,0:T(8,128)(2,1)}, bf16[2,1,512,512]{3,2,1,0:T(8,128)(2,1)}, u32[]{:S(2)}, u32[]{:S(2)}) collective-permute-start(bf16[2,1,512,512]{3,2,1,0:T(8,128)(2,1)} %get-tuple-element.41), channel_id=1, source_target_pairs={{0,8},{8,0},{16,24},{24,16},{1,9},{9,1},{17,25},{25,17},{2,10},{10... | collective-permute-start | bytes 3145736 | tf_op jit(solution)/shard_map/ppermute | solution.py:17
  175.8 36.7 %collective-permute-start.28 = (bf16[2,1,512,512]{3,2,1,0:T(8,128)(2,1)}, bf16[2,1,512,512]{3,2,1,0:T(8,128)(2,1)}, u32[]{:S(2)}, u32[]{:S(2)}) collective-permute-start(bf16[2,1,512,512]{3,2,1,0:T(8,128)(2,1)} %add_convert_fusion.1), channel_id=1, source_target_pairs={{0,16},{8,24},{16,0},{24,8},{1,17},{9,25},{17,1},{25,9},{2,18},{10... | collective-permute-start | bytes 3145736 | tf_op jit(solution)/shard_map/ppermute | solution.py:17
  177.3 37.3 %collective-permute-start.16 = (bf16[128,2048]{1,0:T(8,128)(2,1)S(1)}, bf16[128,2048]{1,0:T(8,128)(2,1)S(1)}, u32[]{:S(2)}, u32[]{:S(2)}) collective-permute-start(bf16[128,2048]{1,0:T(8,128)(2,1)S(1)} %copy-done.22), channel_id=1, source_target_pairs={{0,1},{1,0},{2,3},{3,2},{4,5},{5,4},{6,7},{7,6},{8,9},{9,8},{10,11... | collective-permute-start | bytes 1572872 | tf_op jit(solution)/shard_map/ppermute | solution.py:17
  179.7 35.0 %collective-permute-start.18 = (bf16[128,2048]{1,0:T(8,128)(2,1)S(1)}, bf16[128,2048]{1,0:T(8,128)(2,1)S(1)}, u32[]{:S(2)}, u32[]{:S(2)}) collective-permute-start(bf16[128,2048]{1,0:T(8,128)(2,1)S(1)} %add_convert_fusion.7), channel_id=1, source_target_pairs={{0,4},{1,5},{2,6},{3,7},{4,0},{5,1},{6,2},{7,3},{8,12},{9,13},{10,... | collective-permute-start | bytes 1572872 | tf_op jit(solution)/shard_map/ppermute | solution.py:17
  211.6 13.6 %collective-permute-start.25 = (bf16[1,512,512]{2,1,0:T(8,128)(2,1)S(1)}, bf16[1,512,512]{2,1,0:T(8,128)(2,1)S(1)}, u32[]{:S(2)}, u32[]{:S(2)}) collective-permute-start(bf16[1,512,512]{2,1,0:T(8,128)(2,1)S(1)} %slice.17), channel_id=1, source_target_pairs={{0,16},{8,24},{16,0},{24,8},{1,17},{9,25},{17,1},{25,9},{2,18},{10... | collective-permute-start | bytes 1572872 | tf_op jit(solution)/shard_map/ppermute | solution.py:17
  214.5 13.3 %collective-permute-start.29 = (bf16[512,512]{1,0:T(8,128)(2,1)S(1)}, bf16[512,512]{1,0:T(8,128)(2,1)S(1)}, u32[]{:S(2)}, u32[]{:S(2)}) collective-permute-start(bf16[512,512]{1,0:T(8,128)(2,1)S(1)} %slice_bitcast_fusion), channel_id=1, source_target_pairs={{0,2},{1,3},{2,0},{3,1},{4,6},{5,7},{6,4},{7,5},{8,10},{9,11},{10,... | collective-permute-start | bytes 1572872 | tf_op jit(solution)/shard_map/ppermute | solution.py:17
  (23 other events, 74.8 us)

commit v2 on v0

v2 whole, which is shorter than its diff:
```python
import functools

import jax
import jax.numpy as jnp
from jax import lax
from jax.experimental import pallas as pl
from jax.experimental.pallas import tpu as pltpu
from jax.sharding import PartitionSpec as P

BF16 = jnp.bfloat16
F32 = jnp.float32
VMEM_LIMIT = 60 * 1024 * 1024
TILE = 256
CHUNK = 512

ANY = pl.BlockSpec(memory_space=pl.ANY)
SMEM = pl.BlockSpec(memory_space=pltpu.SMEM)


def swap(value, axis, bit):
    return lax.ppermute(value, axis, [(i, i ^ bit) for i in range(lax.axis_size(axis))])


def bits_of(count):
    return [1 << b for b in reversed(range(count.bit_length() - 1))]


def plus(a, b):
    return (a.astype(F32) + b.astype(F32)).astype(BF16)


def wide(a, b):
    return a.astype(F32) + b.astype(F32)


def dot(a, b, ca=1, cb=0):
    return lax.dot_general(a, b, (((ca,), (cb,)), ((), ())), preferred_element_type=F32)


def shape(*dims):
    return jax.ShapeDtypeStruct(dims, BF16)


def block(index, size):
    return pl.ds(pl.multiple_of(index * size, size), size)


class Copies:
    def __init__(self, sems):
        self.sems = sems
        self.count = 0

    def start(self, src, dst):
        copy = pltpu.make_async_copy(src, dst, self.sems.at[self.count])
        self.count += 1
        copy.start()
        return copy


def wait(copies):
    for copy in copies:
        copy.wait()


def join(arrays, fresh=()):
    n = len(arrays)
    sources, shapes = [], []
    for parts in fresh:
        rows = 0
        for array, first, count, turned in parts:
            if not any(array is x for x in [*arrays, *sources]):
                sources.append(array)
            rows += count
        tail = array.shape[1:][::-1] if turned else array.shape[1:]
        shapes.append(jax.ShapeDtypeStruct((rows, *tail), array.dtype))
    parts = [(i, *p) for i, ps in enumerate(fresh) for p in ps]

    def body(*refs):
        ins = refs[: n + len(sources)]
        outs = refs[len(ins) + n : len(ins) + n + len(fresh)]
        held = refs[len(ins) + n + len(fresh) : -1]
        copies = Copies(refs[-1])
        loads, at = [], {}
        for slot, (i, array, first, count, turned) in zip(held, parts):
            index = next(j for j, x in enumerate([*arrays, *sources]) if x is array)
            loads.append(copies.start(ins[index].at[pl.ds(first, count)], slot))
        wait(loads)
        stores, turns = [], list(held[len(parts) :])
        for slot, (i, array, first, count, turned) in zip(held, parts):
            start = at.get(i, 0)
            at[i] = start + count
            dst = outs[i].at[pl.ds(start, count)]
            if turned:
                turn = turns.pop(0)
                for k in range(count):
                    turn[k] = slot[k].T
                slot = turn
            stores.append(copies.start(slot, dst))
        wait(stores)

    turned = [(c, *a.shape[1:][::-1]) for _, a, _, c, t in parts if t]
    return pl.pallas_call(
        body,
        name="join",
        in_specs=[ANY] * (n + len(sources)),
        out_specs=[ANY] * (n + len(fresh)),
        out_shape=[jax.ShapeDtypeStruct(a.shape, a.dtype) for a in arrays] + shapes,
        input_output_aliases={i: i for i in range(n)},
        scratch_shapes=[pltpu.VMEM((p[3], *p[1].shape[1:]), p[1].dtype) for p in parts]
        + [pltpu.VMEM(dims, BF16) for dims in turned]
        + [pltpu.SemaphoreType.DMA((2 * len(parts) + 1,))],
    )(*arrays, *sources)


def prepare_body(tokens, out_grad, weight_in, weight_out, both, grads, shards, turned, wi, wo, *held):
    rows, wo_t, sems = held[0], held[1], held[-1]
    local = tokens.shape[0]
    copies = Copies(sems)
    loads = [
        copies.start(weight_out, wo),
        copies.start(tokens, rows.at[pl.ds(0, local)]),
        copies.start(out_grad, rows.at[pl.ds(local, local)]),
        copies.start(weight_in, wi),
    ]
    loads[0].wait()
    wo_t[0] = wo[0].T
    stores = [copies.start(wo_t, turned), copies.start(wo_t, shards.at[pl.ds(1, 1)])]
    wait(loads[1:])
    stores.append(copies.start(rows, both))
    stores.append(copies.start(rows.at[pl.ds(local, local)], grads))
    stores.append(copies.start(wi, shards.at[pl.ds(0, 1)]))
    wait(stores)


def prepare(tokens, out_grad, weight_in, weight_out):
    local, width = tokens.shape
    turned = weight_in.shape
    return pl.pallas_call(
        prepare_body,
        name="prepare",
        in_specs=[ANY] * 4,
        out_specs=[ANY] * 4,
        out_shape=[
            shape(2 * local, width),
            shape(local, width),
            shape(2, *turned[1:]),
            shape(*turned),
        ],
        scratch_shapes=[
            pltpu.VMEM(weight_in.shape, BF16),
            pltpu.VMEM(weight_out.shape, BF16),
            pltpu.VMEM((2 * local, width), BF16),
            pltpu.VMEM(turned, BF16),
            pltpu.SemaphoreType.DMA((9,)),
        ],
    )(tokens, out_grad, weight_in, weight_out)


def start_rows(copies, blocks, dst, local):
    return [
        copies.start(ref.at[pl.ds(first, local)], dst.at[pl.ds(i * local, local)])
        for i, (ref, first) in enumerate(blocks)
    ]


def start_weights(copies, pieces, me_d, dst, expert):
    depth = dst.shape[1] // (len(pieces) // 2)
    return [
        copies.start(ref.at[index], dst.at[s, block(me_d ^ m, depth)])
        for (s, m), (ref, index) in sorted(pieces.items())
        if s == expert
    ]


def forward_body(firsts, places, *refs):
    place, refs = refs[0], refs[1:]
    tok, refs = list(zip(refs, firsts)), refs[len(firsts) :]
    count = 1 + max(i for i, _ in places.values())
    pieces = {k: (refs[i], j) for k, (i, j) in places.items()}
    refs = refs[count:]
    act_out, slope_out, t, w, act, slope, sems = refs
    copies = Copies(sems)
    rows_in = start_rows(copies, tok, t, t.shape[0] // len(firsts))
    weights_in = [start_weights(copies, pieces, place[1], w, s) for s in range(2)]
    rows, hidden = t.shape[0], w.shape[2]
    chunk = min(CHUNK, rows)
    wait(rows_in)
    outs = []
    for s in range(2):
        wait(weights_in[s])

        @pl.loop(0, rows // chunk)
        def _(r, s=s):
            some = block(r, chunk)

            @pl.loop(0, hidden // TILE)
            def _(j):
                at = block(j, TILE)
                preact = dot(t[some, :], w[s, :, at])
                logistic = jax.nn.sigmoid(preact)
                act[s, some, at] = (preact * logistic).astype(BF16)
                slope[s, some, at] = (logistic * (1.0 + preact * (1.0 - logistic))).astype(BF16)

        outs.append(copies.start(act.at[s], act_out.at[s]))
        outs.append(copies.start(slope.at[s], slope_out.at[s]))
    wait(outs)


def backward_body(cfg, names, *refs):
    ref = dict(zip(names, refs))
    place = ref["place"]
    me_e, me_d = place[0], place[1]
    local, blocks, share = cfg["local"], cfg["blocks"], cfg["share"]
    pre, act = ref["s_pre"], ref["s_act"]
    hidden = pre.shape[2]
    copies = Copies(ref["sems"])
    g = ref.get("s_g")
    t = ref.get("s_t")
    first = []
    need = {0: [], 1: []}
    later = []
    if cfg["back"]:
        start, count = cfg["back"]
        fresh = range(start // local, (start + count) // local)
        gate, wo, table = ref["s_gate"], ref["s_wo"], ref["s_table"]
        for i in fresh:
            src = ref["grd", i].at[pl.ds(cfg["grd"][i], local)]
            first.append(copies.start(src, g.at[pl.ds(i * local, local)]))
            at = pl.ds(i * local - start, local)
            src = ref["gate", i].at[pl.ds(cfg["gate"][i], local)]
            first.append(copies.start(src, gate.at[at]))
        some = pl.ds(start, count)
        for s in (1, 0):
            pieces = {k: (ref["out", i], j) for k, (i, j) in cfg["out_places"].items()}
            need[s] += start_weights(copies, pieces, me_d, wo, s)
            need[s].append(copies.start(ref["act"].at[s, some], act.at[s, some]))
            need[s].append(copies.start(ref["pre"].at[s, some], pre.at[s, some]))
    else:
        fresh = ()
    if cfg["ins"]:
        later += start_rows(copies, [(ref["tok", i], cfg["tok"][i]) for i in range(blocks)], t, local)
    route_in = []
    if cfg["route"]:
        pieces = {k: (ref["in", i], j) for k, (i, j) in cfg["in_places"].items()}
        route_in = [c for s in range(2) for c in start_weights(copies, pieces, me_d, ref["s_wi"], s)]
    outs = []

    if cfg["back"]:
        start, count = cfg["back"]
        chunk = min(CHUNK, count) if count % min(CHUNK, count) == 0 else local
        gate_lanes = lax.broadcasted_iota(jnp.int32, (chunk, gate.shape[1]), 1)
        wait(first)
        for s in (1, 0):
            wait(need[s])

            @pl.loop(0, count // chunk)
            def _(r, s=s):
                here = block(r, chunk)
                some = pl.ds(pl.multiple_of(start + r * chunk, local), chunk)
                mine = gate_lanes == me_e ^ (share * s)
                weight = jnp.where(mine, gate[here, :].astype(F32), 0.0)
                weight = jnp.sum(weight, axis=1, keepdims=True)

                def step(j, total):
                    at = block(j, TILE)
                    back = dot(g[some, :], wo[s, :, at])
                    value = act[s, some, at].astype(F32)
                    pre[s, some, at] = (weight * pre[s, some, at].astype(F32) * back).astype(BF16)
                    act[s, some, at] = (weight * value).astype(BF16)
                    return total + jnp.sum(value * back, axis=1, keepdims=True)

                column = lax.fori_loop(0, hidden // TILE, step, jnp.zeros((chunk, 1), F32))
                column = jnp.where(mine, column, 0.0).astype(BF16)
                table[here, :] = column if s else table[here, :] + column

        outs.append(copies.start(table, ref["table_out"]))
    wait(later)

    for s in cfg["outs"]:
        stage = ref["s_out"].at[s]
        half, depth = stage.shape[1], stage.shape[3]

        @pl.loop(0, half)
        def _(j, s=s):
            for core in (1, 0):
                at = block(me_d ^ (2 * j + core), depth)
                stage[core, j] = dot(act[s], g[:, at], 0, 0).astype(BF16)

        for core in (1, 0):
            outs.append(copies.start(stage.at[core], ref["out_out", s, core]))

    for high in cfg["ins"]:
        stage = ref["s_in"].at[high]
        n, depth = stage.shape[2:4]

        @pl.loop(0, n)
        def _(j, high=high):
            for core in (1, 0):
                at = block(me_d ^ (2 * (high * n + j) + core), depth)
                for s in range(2):
                    stage[core, s, j] = dot(t[:, at], pre[s], 0, 0).astype(BF16)

        for core in (1, 0):
            outs.append(copies.start(stage.at[core], ref["in_out", high, core]))

    wait(route_in)
    for i in cfg["route"]:
        wi = ref["s_wi"]
        result = ref["s_route"]
        width = result.shape[1]

        @pl.loop(0, width // CHUNK)
        def _(j, i=i):
            at = block(j, CHUNK)
            some = pl.ds(i * local, local)
            total = dot(pre[0, some, :], wi[0, at, :], 1, 1)
            total += dot(pre[1, some, :], wi[1, at, :], 1, 1)
            result[some, at] = total.astype(BF16)

        outs.append(copies.start(result.at[pl.ds(i * local, local)], ref["route_out", i]))
    wait(outs)


def backward_call(cfg, place, held, sizes):
    rows, width, hidden, depth, experts, half = sizes
    local, blocks = cfg["local"], cfg["blocks"]
    wanted, results, scratch = ["place", "pre", "act"], {}, {}
    scratch["s_pre"] = scratch["s_act"] = (2, rows, hidden)
    taken = []
    if cfg["back"]:
        count = cfg["back"][1]
        taken = list(range(cfg["back"][0] // local, sum(cfg["back"]) // local))
        wanted += [("gate", i) for i in taken] + [k for k in held if k[0] == "out"]
        results["table_out"] = scratch["s_table"] = scratch["s_gate"] = (count, experts)
        scratch["s_wo"] = (2, width, hidden)
    if cfg["back"] or cfg["outs"]:
        scratch["s_g"] = (rows, width)
    if cfg["outs"]:
        taken = range(blocks)
        scratch["s_out"] = (2, 2, half, hidden, depth)
        for s in range(2):
            for core in range(2):
                results["out_out", s, core] = scratch["s_out"][2:]
    wanted += [("grd", i) for i in taken]
    if cfg["ins"]:
        wanted += [("tok", i) for i in range(blocks)]
        scratch["s_t"] = (rows, width)
        scratch["s_in"] = (2, 2, 2, half // 2, depth, hidden)
        for high in range(2):
            for core in range(2):
                results["in_out", high, core] = scratch["s_in"][2:]
    if cfg["route"]:
        wanted += [k for k in held if k[0] == "in"]
        scratch["s_wi"] = (2, width, hidden)
        scratch["s_route"] = (rows, width)
        for i in cfg["route"]:
            results["route_out", i] = (local, width)
    names = wanted + list(results) + list(scratch) + ["sems"]
    values = [held[k] for k in wanted[1:]]
    outs = pl.pallas_call(
        functools.partial(backward_body, cfg, names),
        name=cfg["name"],
        in_specs=[SMEM] + [ANY] * len(values),
        out_specs=[ANY] * len(results),
        out_shape=[shape(*dims) for dims in results.values()],
        scratch_shapes=[pltpu.VMEM(dims, BF16) for dims in scratch.values()]
        + [pltpu.SemaphoreType.DMA((2 * len(names) + 4 * blocks,))],
        compiler_params=pltpu.CompilerParams(vmem_limit_bytes=VMEM_LIMIT),
        cost_estimate=pl.CostEstimate(flops=0, bytes_accessed=0, transcendentals=0),
    )(place, *values)
    return dict(zip(results, outs))


def on_device(tokens, out_grad, route_ids, route_gates, weight_in, weight_out):
    local, width = tokens.shape
    experts = lax.axis_size("expert")
    slices = lax.axis_size("dp")
    hidden, depth = weight_in.shape[2], weight_in.shape[1]
    place = jnp.stack([lax.axis_index("expert"), lax.axis_index("dp")]).astype(jnp.int32)

    share = experts // 4
    token_bits = [b for b in bits_of(experts) if b != share]
    dp_bits = bits_of(slices)
    core, others = dp_bits[-1], dp_bits[:-1]

    chosen = route_ids[:, :, None] == jnp.arange(experts, dtype=jnp.int32)
    table = jnp.sum(jnp.where(chosen, route_gates.astype(F32)[:, :, None], 0.0), axis=1).astype(BF16)

    top, rest = token_bits[0], token_bits[1:]
    both, grads, shards, turned = prepare(tokens, out_grad, weight_in, weight_out)
    held = {"tok": tokens, "both": both, "grd": grads, "in": weight_in, "w": shards, "out": turned}
    held["gate"] = table
    tok, grd, gates = {0: "tok"}, {}, {0: "gate"}
    ops = []

    def op(stage, target, source, axis, bit):
        ops.append((stage, target, source, axis, bit))

    for m in range(1, experts):
        low = m & -m
        p = len([b for b in rest if b & m])
        if m & share:
            continue
        if not m & top:
            op(p - 1, ("both", m), ("both", m ^ low) if m ^ low else "both", "expert", low)
        elif m == top:
            op(0, ("tok", m), "tok", "expert", top)
            op(1, ("grd", m), "grd", "expert", top)
            op(0, ("gate", m), "gate", "expert", top)
        else:
            op(p, ("tok", m), ("tok", m ^ low), "expert", low)
            op(p + 1, ("grd", m), ("grd", m ^ low), "expert", low)
    op(0, ("in", 0), "in", "expert", share)
    op(1, ("out", 0), "out", "expert", share)
    for m in range(0, slices, 2):
        low = m & -m
        q = len([b for b in others if b & m])
        if m:
            op(q - 1, ("w", m), ("w", m ^ low) if m ^ low else "w", "dp", low)
            op(q, ("in", m), ("in", m ^ low), "dp", low)
            op(q + 1, ("out", m), ("out", m ^ low), "dp", low)
        op(q, ("w", m | core), ("w", m) if m else "w", "dp", core)
    order = [m for m in range(experts) if not m & share]
    blocks = len(order)
    rows = blocks * local
    half = slices // 2
    sizes = (rows, width, hidden, depth, experts, half)
    keys = [(s, m) for s in range(2) for m in range(slices)]
    pieces = {}
    for m in range(slices):
        for i, kind in enumerate(("in", "out")):
            pieces[kind, 0, m] = (("w", m) if m else "w", i)

    def arrays_of(where):
        names = sorted({name for name, _ in where.values()}, key=str)
        return [held[n] for n in names], {k: (names.index(n), i) for k, (n, i) in where.items()}

    def tok_place(m):
        if m & top or not m:
            return (("tok", m) if m else "tok", 0)
        return (("both", m), 0)

    def grd_place(m):
        if m & top or not m:
            return (("grd", m) if m else "grd", 0)
        return (("both", m), local)

    def forward():
        arrays, at = arrays_of({k[1:]: v for k, v in pieces.items() if k[0] == "in"})
        where = [tok_place(m) for m in order]
        return pl.pallas_call(
            functools.partial(forward_body, [first for _, first in where], at),
            name="forward",
            in_specs=[SMEM] + [ANY] * (blocks + len(arrays)),
            out_specs=[ANY] * 2,
            out_shape=[shape(2, rows, hidden)] * 2,
            scratch_shapes=[
                pltpu.VMEM((rows, width), BF16),
                pltpu.VMEM((2, width, hidden), BF16),
                pltpu.VMEM((2, rows, hidden), BF16),
                pltpu.VMEM((2, rows, hidden), BF16),
                pltpu.SemaphoreType.DMA((blocks + len(at) + 4,)),
            ],
            compiler_params=pltpu.CompilerParams(vmem_limit_bytes=VMEM_LIMIT),
            cost_estimate=pl.CostEstimate(
                flops=4 * rows * width * hidden,
                bytes_accessed=16 * rows * width + 8 * width * hidden,
                transcendentals=0,
            ),
        )(place, *[held[name] for name, _ in where], *arrays)

    last = max(o[0] for o in ops) + 1
    unsent = {(kind, m) for kind in ("in", "out") for m in range(0, slices, 2)}
    gate_where = {0: ("gate", 0)}
    number = 0
    while number <= last or unsent or rest:
        new, pack, bit = [], [], None
        if number:
            passed = [o[1] for o in ops if o[0] == number - 1]
            passed += [k for k in ("pack", "gates") if k in held]
            passed += [k for k in ("grd", "out") if number == 1]
            passed += [k for k in ("act", "pre") if k in held]
            wanted = {o[2] for o in ops if o[0] == number and isinstance(o[2], tuple)}
            passed += [k for k in sorted(wanted, key=str) if k not in passed]
            if number > 1:
                pack = [k for k in sorted(unsent) if k in held]
                unsent -= set(pack)
            if pack:
                new.append([(held[k], 0, 1, False) for k in pack])
            if number > 1 and rest:
                bit, rest = rest[0], rest[1:]
                gate_where[top] = (("gate", top), 0)
                known = sorted(gate_where)
                new.append([(held[n], i, local, False) for n, i in (gate_where[m] for m in known)])
            values = list(join([held[k] for k in passed], new))
            held.update(zip(passed, values))
            new = values[len(passed) :]
        for stage, target, source, axis, b in ops:
            if stage == number:
                held[target] = swap(held[source], axis, b)
        held.pop("pack", None)
        held.pop("gates", None)
        if pack:
            name = ("pack", number)
            held[name] = new.pop(0)
            held[name, core] = swap(held[name], "dp", core)
            for i, (kind, m) in enumerate(pack):
                pieces[kind, 1, m] = ((kind, m), 0)
                pieces[kind, 1, m | core] = ((name, core), i)
        if bit:
            name = ("gates", number)
            held[name] = swap(new.pop(0), "expert", bit)
            for i, m in enumerate(known):
                gate_where[m | bit] = (name, i * local)
        ready = all(("in", s, m) in pieces for s, m in keys)
        ready = ready and all(o[1] in held for o in ops if o[1][0] in ("tok", "both"))
        if ready and "act" not in held:
            held["act"], held["pre"] = forward()
        number += 1

    held["grd"] = out_grad
    named = {"act": held["act"], "pre": held["pre"]}
    cfg = dict(name="backward", local=local, blocks=blocks, share=share)
    cfg.update(back=(0, rows), ins=[1, 0], outs=[1, 0], route=range(blocks))
    for kind in ("in", "out"):
        arrays, cfg[kind + "_places"] = arrays_of({k[1:]: v for k, v in pieces.items() if k[0] == kind})
        named.update({(kind, i): x for i, x in enumerate(arrays)})
    for kind, where in (("tok", tok_place), ("grd", grd_place), ("gate", gate_where.get)):
        cfg[kind] = []
        for i, m in enumerate(order):
            name, first = where(m)
            named[kind, i] = held[name]
            cfg[kind].append(first)
    part = backward_call(cfg, place, named, sizes)
    route = {m: part["route_out", i] for i, m in enumerate(order)}
    (near_keep, near_send), (far_keep, far_send) = (
        [part["out_out", s, c] for c in range(2)] for s in range(2)
    )
    (low_keep, low_send), (high_keep, high_send) = (
        [part["in_out", h, c] for c in range(2)] for h in range(2)
    )
    home = part["table_out"]

    low_bit = token_bits[-1]
    out_far = plus(far_keep, swap(far_send, "dp", core))
    in_far = plus(high_keep, swap(high_send, "dp", core))

    def gates_step(bit):
        sent = [m for m in sorted(home) if m & bit]
        came = swap(jnp.concatenate([home.pop(m) for m in sent], axis=0), "expert", bit)
        for m, one in zip(sent, jnp.split(came, len(sent), axis=0)):
            home[m ^ bit] = plus(home[m ^ bit], one)

    moved = [m for m in sorted(route, reverse=True) if m & low_bit and m != low_bit]
    values = join([out_far, in_far, near_send, low_send] + [route[m] for m in moved])
    out_far, in_far, near_send, low_send = values[:4]
    route.update(zip(moved, values[4:]))
    out_came = swap(out_far, "expert", share)
    in_came = swap(in_far, "dp", others[0])
    near_sum = plus(near_keep, swap(near_send, "dp", core))
    low_sum = plus(low_keep, swap(low_send, "dp", core))
    owned = {}
    for bit in reversed(token_bits[1:]):
        for m in sorted(route, reverse=True):
            if m == bit:
                owned[m] = route.pop(m)
            elif m & bit:
                route[m ^ bit] = plus(route[m ^ bit], swap(route.pop(m), "expert", bit))
    sent = list(owned)
    values = join([route[top], home, near_sum, low_sum, *owned.values()])
    route[top], home, near_sum, low_sum = values[:4]
    owned = {m: swap(v, "expert", m) for m, v in zip(sent, values[4:])}
    owned[top] = swap(route[top], "expert", top)
    home = dict(zip(order, jnp.split(home, blocks, axis=0)))
    for bit in reversed(token_bits):
        gates_step(bit)
    total = route[0].astype(F32)
    for came in owned.values():
        total += came.astype(F32)
    grad_tokens = total.astype(BF16)
    grad_gates = jnp.sum(jnp.where(chosen, home[0].astype(F32)[:, None, :], 0.0), axis=2)

    in_sum = plus(low_sum, in_came)
    for bit in others[1:]:
        n = in_sum.shape[1] // 2
        in_sum = plus(in_sum[:, :n], swap(in_sum[:, n:], "dp", bit))
    grad_in = wide(in_sum[0, 0], swap(in_sum[1, 0], "expert", share))

    out_sum = plus(near_sum, out_came)
    for bit in others:
        n = out_sum.shape[0] // 2
        total = wide if bit == others[-1] else plus
        out_sum = total(out_sum[:n], swap(out_sum[n:], "dp", bit))
    return (grad_tokens, grad_gates.astype(BF16), grad_in[None], out_sum)


def solution(mesh):
    return jax.shard_map(
        on_device,
        mesh=mesh,
        in_specs=(
            P(("dp", "expert"), None),
            P(("dp", "expert"), None),
            P(("dp", "expert"), None),
            P(("dp", "expert"), None),
            P("expert", "dp", None),
            P("expert", None, "dp"),
        ),
        out_specs=(
            P(("dp", "expert"), None),
            P(("dp", "expert"), None),
            P("expert", "dp", None),
            P("expert", None, "dp"),
        ),
        check_vma=False,
    )
```

time: 228 us -> 181 us (0.79)
  waiting for transfers between devices: 134 us -> 84.1 us
  Pallas kernels: 0 us -> 36.3 us
  matrix products: 18.9 us -> 0 us
  local copies, waits for them, and re-layouts: 24.2 us -> 8.02 us
  between operations: 14 us -> 0.93 us
  starting transfers between devices: 24.5 us -> 34.6 us
  other arithmetic: 11 us -> 16 us
    all_to_all x5 -> x0, waiting for transfers between devices: 112 us -> none  [the longest x1 46.9 us: on_device(): lax.all_to_all(outbound_inputs, 'expert', split_axis=0, concat_axis=0, ti...]
    ppermute x0 -> x29, waiting for transfers between devices: none -> 84.1 us  [swap(): lax.ppermute(value, axis, [(i, i ^ bit) for i in range(lax.axis_size(axis...]
    pallas_call x0 -> x8, Pallas kernels: none -> 36.3 us  [the longest x1 21.7 us: backward_call(): pl.pallas_call(functools.partial(backward_body, cfg, names), name=cfg['na...]
    ppermute x0 -> x29, starting transfers between devices: none -> 34.6 us  [swap(): lax.ppermute(value, axis, [(i, i ^ bit) for i in range(lax.axis_size(axis...]
    all_to_all x5 -> x0, starting transfers between devices: 24.1 us -> none  [the longest x1 7.25 us: on_device(): lax.all_to_all(outbound_gates, 'expert', split_axis=0, concat_axis=0, til...]
    all_gather x2 -> x0, waiting for transfers between devices: 21.1 us -> none  [the longest x1 21.1 us: on_device(): lax.all_gather(weight_out, 'dp', axis=2, tiled=True)]
    dot_general x5 -> x0, matrix products: 18.9 us -> none  [the longest x1 4.74 us: backward_rows(): lax.dot_general(hidden_act, scaled, (((0,), (0,)), ((), ())), preferred_e...]
    gather x5 -> x0, local copies, waits for them, and re-layouts: 13.4 us -> none  [the longest x1 3.36 us: on_device(): jnp.take(route_gates.reshape(-1), route_of_slot, axis=0, mode='fill', fil...]
  transfers between devices with their start and end apart: 9 -> 29, of which waited for: 5 -> 15; matrix products, arithmetic and copies ran while one was open for 15% -> 8% of each run, Pallas kernels for 0% -> 4%
where the time goes in v2:
time: 181 us; the launch traced here: 180 us
  waiting for transfers between devices  84.1 us (46%)
  Pallas kernels  36.3 us (20%)
  starting transfers between devices  34.6 us (19%)
  other arithmetic  16 us (9%)
  local copies, waits for them, and re-layouts  8.02 us (4%)
    ppermute x29, waiting for transfers between devices, swap(): lax.ppermute(value, axis, [(i, i ^ bit) for i in range(lax.axis_size(axis...  84.1 us
    ppermute x29, starting transfers between devices, swap(): lax.ppermute(value, axis, [(i, i ^ bit) for i in range(lax.axis_size(axis...  34.6 us
    pallas_call x1, Pallas kernels, backward_call(): pl.pallas_call(functools.partial(backward_body, cfg, names), name=cfg['na...  21.7 us
    convert_element_type x8, other arithmetic, plus(): return (a.astype(F32) + b.astype(F32)).astype(BF16)  9.34 us
    pallas_call x1, Pallas kernels, forward(): pl.pallas_call(functools.partial(forward_body, [first for _, first in whe...  6.98 us
    unnamed x54, local copies, waits for them, and re-layouts  6.2 us
    pallas_call x5, Pallas kernels, join(): pl.pallas_call(body, name='join', in_specs=[ANY] * (n + len(sources)), ou...  4.6 us
  transfers between devices with their start and end apart: 29, of which 15 were waited for; matrix products, arithmetic and copies ran while one was open for 8% of the time, Pallas kernels for 4%

profile of v2, /device:TPU:0, one launch (start us, length us, event | category | flops | bytes accessed | tf_op | source)
XLA Modules:
  0.0 180.0 jit_solution(5264344338220001111)
XLA Ops:
  0.7 3.0 %prepare.1 = (bf16[256,2048]{1,0:T(8,128)(2,1)}, bf16[128,2048]{1,0:T(8,128)(2,1)}, bf16[2,512,512]{2,1,0:T(8,128)(2,1)}, bf16[1,512,512]{2,1,0:T(8,128)(2,1)}) custom-call(bf16[128,2048]{1,0:T(8,128)(2,1)} %refs_19_.1, bf16[128,2048]{1,0:T(8,128)(2,1)} %refs_15_.1, bf16[1,512,512]{2,1,0:T(8,128)(2,1)} %weight_in.1, bf16[1,512,512]{2,1,0:T(8,128)(2,1)} %weight_out.1), custom_call_target="tpu_custom_call" | custom-call | tf_op jit(solution)/shard_map/prepare/pallas_call | solution.py:138
  3.6 3.0 %collective-permute-start = (bf16[256,2048]{1,0:T(8,128)(2,1)}, bf16[256,2048]{1,0:T(8,128)(2,1)S(1)}, u32[]{:S(2)}, u32[]{:S(2)}) collective-permute-start(bf16[256,2048]{1,0:T(8,128)(2,1)} %get-tuple-element.53), channel_id=1, source_target_pairs={{0,1},{1,0},{2,3},{3,2},{4,5},{5,4},{6,7},{7,6},{8,9},{9,8},{10,11... | collective-permute-start | bytes 3145736 | tf_op jit(solution)/shard_map/ppermute | solution.py:21
  6.6 1.5 collective-permute-start.5
  8.3 2.7 %collective-permute-start.2 = (bf16[128,8]{1,0:T(8,128)(2,1)S(1)}, bf16[128,8]{1,0:T(8,128)(2,1)S(1)}, u32[]{:S(2)}, u32[]{:S(2)}) collective-permute-start(bf16[128,8]{1,0:T(8,128)(2,1)S(1)} %copy.46.refs_6_.refs_3_), channel_id=1, source_target_pairs={{0,4},{1,5},{2,6},{3,7},{4,0},{5,1},{6,2},{7,3},{8,12},{9,13},{10,... | collective-permute-start | bytes 6152 | tf_op jit(solution)/shard_map/ppermute | solution.py:21
  11.0 1.6 collective-permute-start.3
  13.2 2.6 %collective-permute-start.1 = (bf16[128,2048]{1,0:T(8,128)(2,1)}, bf16[128,2048]{1,0:T(8,128)(2,1)S(1)}, u32[]{:S(2)}, u32[]{:S(2)}) collective-permute-start(bf16[128,2048]{1,0:T(8,128)(2,1)} %refs_19_.1), channel_id=1, source_target_pairs={{0,4},{1,5},{2,6},{3,7},{4,0},{5,1},{6,2},{7,3},{8,12},{9,13},{10,... | collective-permute-start | bytes 1572872 | tf_op jit(solution)/shard_map/ppermute | solution.py:21
  15.8 18.6 %collective-permute-done.3.refs_3_ = bf16[1,512,512]{2,1,0:T(8,128)(2,1)S(1)} collective-permute-done((bf16[1,512,512]{2,1,0:T(8,128)(2,1)}, bf16[1,512,512]{2,1,0:T(8,128)(2,1)S(1)}, u32[]{:S(2)}, u32[]{:S(2)}) %collective-permute-start.3) | collective-permute-done | bytes 524320 | tf_op jit(solution)/shard_map/ppermute | solution.py:21
  34.4 4.4 %collective-permute-done.1.refs_1_ = bf16[128,2048]{1,0:T(8,128)(2,1)S(1)} collective-permute-done((bf16[128,2048]{1,0:T(8,128)(2,1)}, bf16[128,2048]{1,0:T(8,128)(2,1)S(1)}, u32[]{:S(2)}, u32[]{:S(2)}) %collective-permute-start.1) | collective-permute-done | bytes 524320 | tf_op jit(solution)/shard_map/ppermute | solution.py:21
  41.0 5.0 %collective-permute-start.8 = (bf16[1,512,512]{2,1,0:T(8,128)(2,1)}, bf16[1,512,512]{2,1,0:T(8,128)(2,1)S(1)}, u32[]{:S(2)}, u32[]{:S(2)}) collective-permute-start(bf16[1,512,512]{2,1,0:T(8,128)(2,1)} %get-tuple-element.59), channel_id=1, source_target_pairs={{0,2},{1,3},{2,0},{3,1},{4,6},{5,7},{6,4},{7,5},{8,10},{9,11},{10,... | collective-permute-start | bytes 1572872 | tf_op jit(solution)/shard_map/ppermute | solution.py:21
  47.1 20.4 %collective-permute-done.6.refs_0_ = bf16[128,2048]{1,0:T(8,128)(2,1)S(1)} collective-permute-done((bf16[128,2048]{1,0:T(8,128)(2,1)}, bf16[128,2048]{1,0:T(8,128)(2,1)S(1)}, u32[]{:S(2)}, u32[]{:S(2)}) %collective-permute-start.6) | collective-permute-done | bytes 524320 | tf_op jit(solution)/shard_map/ppermute | solution.py:21
  69.2 2.7 %join.6 = (bf16[128,2048]{1,0:T(8,128)(2,1)}, bf16[128,2048]{1,0:T(8,128)(2,1)}, bf16[1,512,512]{2,1,0:T(8,128)(2,1)}, bf16[1,512,512]{2,1,0:T(8,128)(2,1)}, bf1...) custom-call(bf16[128,2048]{1,0:T(8,128)(2,1)} %copy-done.10, ...), custom_call_target="tpu_custom_call", output_to_operand_aliasing={{0}: (0, {}), {1}: (1, {}), {2}: (2, {}), {3}: (3, {}), {4}... | custom-call | tf_op jit(solution)/shard_map/join/pallas_call | solution.py:102
  74.0 1.5 collective-permute-done.13.refs_10_.refs_12_.refs_28_
  76.7 7.0 %forward.1 = (bf16[2,512,512]{2,1,0:T(8,128)(2,1)}, bf16[2,512,512]{2,1,0:T(8,128)(2,1)}) custom-call(s32[2]{0:T(128)} %pad_add_fusion.refs_0_, bf16[128,2048]{1,0:T(8,128)(2,1)} %refs_19_.1, bf16[256,2048]{1,0:T(8,128)(2,1)} %get-tuple-element.65.refs_2_.refs_16_.refs_20_, bf16[128,2048]{1,0:T(8,128)(2,1)} %get-tuple-element.58.refs_3_.refs_21_, ...), custom_call_target="tpu_custom_call" | custom-call | flops 2147483648 | bytes 25165824 | tf_op jit(solution)/shard_map/forward/pallas_call | solution.py:451
  83.7 2.8 %collective-permute-done.11.refs_0_ = bf16[128,2048]{1,0:T(8,128)(2,1)S(1)} collective-permute-done((bf16[128,2048]{1,0:T(8,128)(2,1)}, bf16[128,2048]{1,0:T(8,128)(2,1)S(1)}, u32[]{:S(2)}, u32[]{:S(2)}) %collective-permute-start.11) | collective-permute-done | bytes 524320 | tf_op jit(solution)/shard_map/ppermute | solution.py:21
  87.6 1.9 %join.7 = (bf16[128,2048]{1,0:T(8,128)(2,1)}, bf16[1,512,512]{2,1,0:T(8,128)(2,1)}, bf16[2,512,512]{2,1,0:T(8,128)(2,1)}, bf16[2,512,512]{2,1,0:T(8,128)(2,1)}, bf16[1,512,512]{2,1,0:T(8,128)(2,1)}) custom-call(bf16[128,2048]{1,0:T(8,128)(2,1)} %copy-done.12, ...), custom_call_target="tpu_custom_call", output_to_operand_aliasing={{0}: (0, {}), {1}: (1, {}), {2}: (2, {}), {3}: (3, {})} | custom-call | tf_op jit(solution)/shard_map/join/pallas_call | solution.py:102
  89.6 1.6 collective-permute-start.14
  91.1 2.9 %collective-permute-done.14.refs_4_.refs_6_ = bf16[256,8]{1,0:T(8,128)(2,1)S(1)} collective-permute-done((bf16[256,8]{1,0:T(8,128)(2,1)S(1)}, bf16[256,8]{1,0:T(8,128)(2,1)S(1)}, u32[]{:S(2)}, u32[]{:S(2)}) %collective-permute-start.14) | collective-permute-done | bytes 4128 | tf_op jit(solution)/shard_map/ppermute | solution.py:21
  94.9 21.7 %backward.1 = (bf16[512,8]{1,0:T(8,128)(2,1)}, bf16[2,512,512]{2,1,0:T(8,128)(2,1)}, bf16[2,512,512]{2,1,0:T(8,128)(2,1)}, bf16[2,512,512]{2,1,0:T(8,128)(2,1)},...) custom-call(s32[2]{0:T(128)} %pad_add_fusion.refs_0_, ...), custom_call_target="tpu_custom_call" | custom-call | tf_op jit(solution)/shard_map/backward/pallas_call | solution.py:360
  117.2 2.4 %collective-permute-done.16 = bf16[2,512,512]{2,1,0:T(8,128)(2,1)S(1)} collective-permute-done((bf16[2,512,512]{2,1,0:T(8,128)(2,1)}, bf16[2,512,512]{2,1,0:T(8,128)(2,1)S(1)}, u32[]{:S(2)}, u32[]{:S(2)}) %collective-permute-start.16) | collective-permute-done | bytes 1048608 | tf_op jit(solution)/shard_map/ppermute | solution.py:21
  119.6 2.6 %add_convert_fusion.5.refs_0_ = bf16[2,512,512]{2,1,0:T(8,128)(2,1)} fusion(bf16[2,512,512]{2,1,0:T(8,128)(2,1)S(1)} %collective-permute-done.16, bf16[2,512,512]{2,1,0:T(8,128)(2,1)} %get-tuple-element.81), kind=kLoop, calls=%fused_computation.5 | loop fusion | flops 2097152 | bytes 3145728 | tf_op jit(solution)/shard_map/convert_element_type | solution.py:29
  123.7 1.5 collective-permute-start.18
  125.8 12.3 %collective-permute-done.18 = bf16[128,2048]{1,0:T(8,128)(2,1)S(1)} collective-permute-done((bf16[128,2048]{1,0:T(8,128)(2,1)}, bf16[128,2048]{1,0:T(8,128)(2,1)S(1)}, u32[]{:S(2)}, u32[]{:S(2)}) %collective-permute-start.18) | collective-permute-done | bytes 524320 | tf_op jit(solution)/shard_map/ppermute | solution.py:21
  142.5 1.6 collective-permute-start.23
  144.6 2.4 %collective-permute-start.22 = (bf16[128,2048]{1,0:T(8,128)(2,1)}, bf16[128,2048]{1,0:T(8,128)(2,1)}, u32[]{:S(2)}, u32[]{:S(2)}) collective-permute-start(bf16[128,2048]{1,0:T(8,128)(2,1)} %get-tuple-element.96), channel_id=1, source_target_pairs={{0,4},{1,5},{2,6},{3,7},{4,0},{5,1},{6,2},{7,3},{8,12},{9,13},{10,... | collective-permute-start | bytes 1572872 | tf_op jit(solution)/shard_map/ppermute | solution.py:21
  146.9 4.1 %collective-permute-done.25 = bf16[2,1,512,512]{3,2,1,0:T(8,128)(2,1)S(1)} collective-permute-done((bf16[2,1,512,512]{3,2,1,0:T(8,128)(2,1)}, bf16[2,1,512,512]{3,2,1,0:T(8,128)(2,1)S(1)}, u32[]{:S(2)}, u32[]{:S(2)}) %collective-permute-start.25) | collective-permute-done | bytes 1048608 | tf_op jit(solution)/shard_map/ppermute | solution.py:21
  151.0 1.6 add_convert_fusion.1
  153.5 4.1 %collective-permute-start.24 = (bf16[128,8]{1,0:T(8,128)(2,1)S(1)}, bf16[128,8]{1,0:T(8,128)(2,1)S(1)}, u32[]{:S(2)}, u32[]{:S(2)}) collective-permute-start(bf16[128,8]{1,0:T(8,128)(2,1)S(1)} %add_convert_fusion.9), channel_id=1, source_target_pairs={{0,4},{1,5},{2,6},{3,7},{4,0},{5,1},{6,2},{7,3},{8,12},{9,13},{10,... | collective-permute-start | bytes 6152 | tf_op jit(solution)/shard_map/ppermute | solution.py:21
  158.1 2.2 %collective-permute-start.28 = (bf16[1,512,512]{2,1,0:T(8,128)(2,1)S(1)}, bf16[1,512,512]{2,1,0:T(8,128)(2,1)S(1)}, u32[]{:S(2)}, u32[]{:S(2)}) collective-permute-start(bf16[1,512,512]{2,1,0:T(8,128)(2,1)S(1)} %slice.19), channel_id=1, source_target_pairs={{0,16},{8,24},{16,0},{24,8},{1,17},{9,25},{17,1},{25,9},{2,18},{10... | collective-permute-start | bytes 1572872 | tf_op jit(solution)/shard_map/ppermute | solution.py:21
  160.4 11.9 %collective-permute-done.24 = bf16[128,8]{1,0:T(8,128)(2,1)S(1)} collective-permute-done((bf16[128,8]{1,0:T(8,128)(2,1)S(1)}, bf16[128,8]{1,0:T(8,128)(2,1)S(1)}, u32[]{:S(2)}, u32[]{:S(2)}) %collective-permute-start.24) | collective-permute-done | bytes 2080 | tf_op jit(solution)/shard_map/ppermute | solution.py:21
  172.9 1.6 collective-permute-done.26
  174.5 2.2 %fusion = f32[1,512,512]{2,1,0:T(8,128)} fusion(bf16[512,512]{1,0:T(8,128)(2,1)} %collective-permute-done.26, bf16[2,1,512,512]{3,2,1,0:T(8,128)(2,1)S(1)} %add_convert_fusion.1), kind=kLoop, calls=%fused_computation.7 | loop fusion | flops 786432 | bytes 2097152 | tf_op jit(solution)/shard_map/broadcast_in_dim | solution.py:594
  177.8 2.2 %add_convert_fusion.6 = bf16[128,2048]{1,0:T(8,128)(2,1)} fusion(bf16[128,2048]{1,0:T(8,128)(2,1)} %collective-permute-done.22, bf16[128,2048]{1,0:T(8,128)(2,1)} %collective-permute-done.21, bf16[128,2048]{1,0:T(8,128)(2,1)S(1)} %copy-done.20), kind=kLoop, calls=%fused_computation.9 | loop fusion | flops 1572864 | bytes 2097152 | tf_op jit(solution)/shard_map/convert_element_type | solution.py:580
  (110 shorter events, 21.7 us)
Async XLA Ops:
  3.6 35.1 %collective-permute-start = (bf16[256,2048]{1,0:T(8,128)(2,1)}, bf16[256,2048]{1,0:T(8,128)(2,1)S(1)}, u32[]{:S(2)}, u32[]{:S(2)}) collective-permute-start(bf16[256,2048]{1,0:T(8,128)(2,1)} %get-tuple-element.53), channel_id=1, source_target_pairs={{0,1},{1,0},{2,3},{3,2},{4,5},{5,4},{6,7},{7,6},{8,9},{9,8},{10,11... | collective-permute-start | bytes 3145736 | tf_op jit(solution)/shard_map/ppermute | solution.py:21
  6.6 32.1 %collective-permute-start.5 = (bf16[2,512,512]{2,1,0:T(8,128)(2,1)}, bf16[2,512,512]{2,1,0:T(8,128)(2,1)S(1)}, u32[]{:S(2)}, u32[]{:S(2)}) collective-permute-start(bf16[2,512,512]{2,1,0:T(8,128)(2,1)} %get-tuple-element.54.refs_11_.refs_14_.refs_29_), channel_id=1, source_target_pairs={{0,16},{8,24},{16,0},{24,8},{1,17},{9,25},{17,1},{25,9},{2,18},{10... | collective-permute-start | bytes 3145736 | tf_op jit(solution)/shard_map/ppermute | solution.py:21
  8.2 30.6 %collective-permute-start.4 = (bf16[2,512,512]{2,1,0:T(8,128)(2,1)}, bf16[2,512,512]{2,1,0:T(8,128)(2,1)S(1)}, u32[]{:S(2)}, u32[]{:S(2)}) collective-permute-start(bf16[2,512,512]{2,1,0:T(8,128)(2,1)} %get-tuple-element.54.refs_11_.refs_14_.refs_29_), channel_id=1, source_target_pairs={{0,8},{8,0},{16,24},{24,16},{1,9},{9,1},{17,25},{25,17},{2,10},{10... | collective-permute-start | bytes 3145736 | tf_op jit(solution)/shard_map/ppermute | solution.py:21
  8.3 59.3 %copy-start.22 = (bf16[128,8]{1,0:T(8,128)(2,1)}, bf16[128,8]{1,0:T(8,128)(2,1)S(1)}, u32[]{:S(2)}) copy-start(bf16[128,8]{1,0:T(8,128)(2,1)S(1)} %copy.46.refs_6_.refs_3_) | copy-start | bytes 6148
  8.3 4.9 %collective-permute-start.2 = (bf16[128,8]{1,0:T(8,128)(2,1)S(1)}, bf16[128,8]{1,0:T(8,128)(2,1)S(1)}, u32[]{:S(2)}, u32[]{:S(2)}) collective-permute-start(bf16[128,8]{1,0:T(8,128)(2,1)S(1)} %copy.46.refs_6_.refs_3_), channel_id=1, source_target_pairs={{0,4},{1,5},{2,6},{3,7},{4,0},{5,1},{6,2},{7,3},{8,12},{9,13},{10,... | collective-permute-start | bytes 6152 | tf_op jit(solution)/shard_map/ppermute | solution.py:21
  11.0 23.4 %collective-permute-start.3 = (bf16[1,512,512]{2,1,0:T(8,128)(2,1)}, bf16[1,512,512]{2,1,0:T(8,128)(2,1)S(1)}, u32[]{:S(2)}, u32[]{:S(2)}) collective-permute-start(bf16[1,512,512]{2,1,0:T(8,128)(2,1)} %weight_in.1), channel_id=1, source_target_pairs={{0,2},{1,3},{2,0},{3,1},{4,6},{5,7},{6,4},{7,5},{8,10},{9,11},{10,... | collective-permute-start | bytes 1572872 | tf_op jit(solution)/shard_map/ppermute | solution.py:21
  13.2 26.4 %copy-start.21 = (bf16[128,8]{1,0:T(8,128)(2,1)}, bf16[128,8]{1,0:T(8,128)(2,1)S(1)}, u32[]{:S(2)}) copy-start(bf16[128,8]{1,0:T(8,128)(2,1)S(1)} %collective-permute-done.2.refs_2_) | copy-start | bytes 6148
  13.2 25.6 %collective-permute-start.1 = (bf16[128,2048]{1,0:T(8,128)(2,1)}, bf16[128,2048]{1,0:T(8,128)(2,1)S(1)}, u32[]{:S(2)}, u32[]{:S(2)}) collective-permute-start(bf16[128,2048]{1,0:T(8,128)(2,1)} %refs_19_.1), channel_id=1, source_target_pairs={{0,4},{1,5},{2,6},{3,7},{4,0},{5,1},{6,2},{7,3},{8,12},{9,13},{10,... | collective-permute-start | bytes 1572872 | tf_op jit(solution)/shard_map/ppermute | solution.py:21
  40.6 27.0 %collective-permute-start.10 = (bf16[2,512,512]{2,1,0:T(8,128)(2,1)}, bf16[2,512,512]{2,1,0:T(8,128)(2,1)S(1)}, u32[]{:S(2)}, u32[]{:S(2)}) collective-permute-start(bf16[2,512,512]{2,1,0:T(8,128)(2,1)} %get-tuple-element.61.refs_8_.refs_10_.refs_26_), channel_id=1, source_target_pairs={{0,8},{8,0},{16,24},{24,16},{1,9},{9,1},{17,25},{25,17},{2,10},{10... | collective-permute-start | bytes 3145736 | tf_op jit(solution)/shard_map/ppermute | solution.py:21
  40.7 26.8 %collective-permute-start.6 = (bf16[128,2048]{1,0:T(8,128)(2,1)}, bf16[128,2048]{1,0:T(8,128)(2,1)S(1)}, u32[]{:S(2)}, u32[]{:S(2)}) collective-permute-start(bf16[128,2048]{1,0:T(8,128)(2,1)} %get-tuple-element.57), channel_id=1, source_target_pairs={{0,4},{1,5},{2,6},{3,7},{4,0},{5,1},{6,2},{7,3},{8,12},{9,13},{10,... | collective-permute-start | bytes 1572872 | tf_op jit(solution)/shard_map/ppermute | solution.py:21
  41.0 26.5 %collective-permute-start.8 = (bf16[1,512,512]{2,1,0:T(8,128)(2,1)}, bf16[1,512,512]{2,1,0:T(8,128)(2,1)S(1)}, u32[]{:S(2)}, u32[]{:S(2)}) collective-permute-start(bf16[1,512,512]{2,1,0:T(8,128)(2,1)} %get-tuple-element.59), channel_id=1, source_target_pairs={{0,2},{1,3},{2,0},{3,1},{4,6},{5,7},{6,4},{7,5},{8,10},{9,11},{10,... | collective-permute-start | bytes 1572872 | tf_op jit(solution)/shard_map/ppermute | solution.py:21
  46.0 21.6 %collective-permute-start.7 = (bf16[128,2048]{1,0:T(8,128)(2,1)}, bf16[128,2048]{1,0:T(8,128)(2,1)S(1)}, u32[]{:S(2)}, u32[]{:S(2)}) collective-permute-start(bf16[128,2048]{1,0:T(8,128)(2,1)} %get-tuple-element.58.refs_3_.refs_21_), channel_id=1, source_target_pairs={{0,1},{1,0},{2,3},{3,2},{4,5},{5,4},{6,7},{7,6},{8,9},{9,8},{10,11... | collective-permute-start | bytes 1572872 | tf_op jit(solution)/shard_map/ppermute | solution.py:21
  46.6 21.0 %collective-permute-start.9 = (bf16[1,512,512]{2,1,0:T(8,128)(2,1)}, bf16[1,512,512]{2,1,0:T(8,128)(2,1)S(1)}, u32[]{:S(2)}, u32[]{:S(2)}) collective-permute-start(bf16[1,512,512]{2,1,0:T(8,128)(2,1)} %get-tuple-element.60.refs_5_.refs_23_), channel_id=1, source_target_pairs={{0,16},{8,24},{16,0},{24,8},{1,17},{9,25},{17,1},{25,9},{2,18},{10... | collective-permute-start | bytes 1572872 | tf_op jit(solution)/shard_map/ppermute | solution.py:21
  71.9 3.7 %collective-permute-start.13 = (bf16[3,512,512]{2,1,0:T(8,128)(2,1)}, bf16[3,512,512]{2,1,0:T(8,128)(2,1)S(1)}, u32[]{:S(2)}, u32[]{:S(2)}) collective-permute-start(bf16[3,512,512]{2,1,0:T(8,128)(2,1)} %get-tuple-element.70), channel_id=1, source_target_pairs={{0,8},{8,0},{16,24},{24,16},{1,9},{9,1},{17,25},{25,17},{2,10},{10... | collective-permute-start | bytes 4718600 | tf_op jit(solution)/shard_map/ppermute | solution.py:21
  72.0 14.6 %collective-permute-start.11 = (bf16[128,2048]{1,0:T(8,128)(2,1)}, bf16[128,2048]{1,0:T(8,128)(2,1)S(1)}, u32[]{:S(2)}, u32[]{:S(2)}) collective-permute-start(bf16[128,2048]{1,0:T(8,128)(2,1)} %get-tuple-element.63.refs_17_), channel_id=1, source_target_pairs={{0,1},{1,0},{2,3},{3,2},{4,5},{5,4},{6,7},{7,6},{8,9},{9,8},{10,11... | collective-permute-start | bytes 1572872 | tf_op jit(solution)/shard_map/ppermute | solution.py:21
  72.6 14.2 %collective-permute-start.12 = (bf16[1,512,512]{2,1,0:T(8,128)(2,1)}, bf16[1,512,512]{2,1,0:T(8,128)(2,1)S(1)}, u32[]{:S(2)}, u32[]{:S(2)}) collective-permute-start(bf16[1,512,512]{2,1,0:T(8,128)(2,1)} %get-tuple-element.64.refs_7_), channel_id=1, source_target_pairs={{0,16},{8,24},{16,0},{24,8},{1,17},{9,25},{17,1},{25,9},{2,18},{10... | collective-permute-start | bytes 1572872 | tf_op jit(solution)/shard_map/ppermute | solution.py:21
  89.5 4.6 %collective-permute-start.15 = (bf16[1,512,512]{2,1,0:T(8,128)(2,1)}, bf16[1,512,512]{2,1,0:T(8,128)(2,1)S(1)}, u32[]{:S(2)}, u32[]{:S(2)}) collective-permute-start(bf16[1,512,512]{2,1,0:T(8,128)(2,1)} %get-tuple-element.77), channel_id=1, source_target_pairs={{0,8},{8,0},{16,24},{24,16},{1,9},{9,1},{17,25},{25,17},{2,10},{10... | collective-permute-start | bytes 1572872 | tf_op jit(solution)/shard_map/ppermute | solution.py:21
  89.6 4.5 %collective-permute-start.14 = (bf16[256,8]{1,0:T(8,128)(2,1)S(1)}, bf16[256,8]{1,0:T(8,128)(2,1)S(1)}, u32[]{:S(2)}, u32[]{:S(2)}) collective-permute-start(bf16[256,8]{1,0:T(8,128)(2,1)S(1)} %copy-done.25), channel_id=1, source_target_pairs={{0,1},{1,0},{2,3},{3,2},{4,5},{5,4},{6,7},{7,6},{8,9},{9,8},{10,11... | collective-permute-start | bytes 12296 | tf_op jit(solution)/shard_map/ppermute | solution.py:21
  116.6 2.9 %collective-permute-start.16 = (bf16[2,512,512]{2,1,0:T(8,128)(2,1)}, bf16[2,512,512]{2,1,0:T(8,128)(2,1)S(1)}, u32[]{:S(2)}, u32[]{:S(2)}) collective-permute-start(bf16[2,512,512]{2,1,0:T(8,128)(2,1)} %get-tuple-element.82), channel_id=1, source_target_pairs={{0,8},{8,0},{16,24},{24,16},{1,9},{9,1},{17,25},{25,17},{2,10},{10... | collective-permute-start | bytes 3145736 | tf_op jit(solution)/shard_map/ppermute | solution.py:21
  116.7 5.4 %collective-permute-start.17 = (bf16[2,1,512,512]{3,2,1,0:T(8,128)(2,1)}, bf16[2,1,512,512]{3,2,1,0:T(8,128)(2,1)S(1)}, u32[]{:S(2)}, u32[]{:S(2)}) collective-permute-start(bf16[2,1,512,512]{3,2,1,0:T(8,128)(2,1)} %get-tuple-element.84), channel_id=1, source_target_pairs={{0,8},{8,0},{16,24},{24,16},{1,9},{9,1},{17,25},{25,17},{2,10},{10... | collective-permute-start | bytes 3145736 | tf_op jit(solution)/shard_map/ppermute | solution.py:21
  123.5 15.6 %copy-start.15 = (bf16[2,512,512]{2,1,0:T(8,128)(2,1)S(1)}, bf16[2,512,512]{2,1,0:T(8,128)(2,1)}, u32[]{:S(2)}) copy-start(bf16[2,512,512]{2,1,0:T(8,128)(2,1)} %get-tuple-element.90) | copy-start | bytes 3145732
  123.5 15.5 %collective-permute-start.19 = (bf16[2,512,512]{2,1,0:T(8,128)(2,1)}, bf16[2,512,512]{2,1,0:T(8,128)(2,1)S(1)}, u32[]{:S(2)}, u32[]{:S(2)}) collective-permute-start(bf16[2,512,512]{2,1,0:T(8,128)(2,1)} %get-tuple-element.91), channel_id=1, source_target_pairs={{0,8},{8,0},{16,24},{24,16},{1,9},{9,1},{17,25},{25,17},{2,10},{10... | collective-permute-start | bytes 3145736 | tf_op jit(solution)/shard_map/ppermute | solution.py:21
  123.7 14.4 %collective-permute-start.18 = (bf16[128,2048]{1,0:T(8,128)(2,1)}, bf16[128,2048]{1,0:T(8,128)(2,1)S(1)}, u32[]{:S(2)}, u32[]{:S(2)}) collective-permute-start(bf16[128,2048]{1,0:T(8,128)(2,1)} %get-tuple-element.88), channel_id=1, source_target_pairs={{0,1},{1,0},{2,3},{3,2},{4,5},{5,4},{6,7},{7,6},{8,9},{9,8},{10,11... | collective-permute-start | bytes 1572872 | tf_op jit(solution)/shard_map/ppermute | solution.py:21
  125.2 15.2 %collective-permute-start.20 = (bf16[2,1,512,512]{3,2,1,0:T(8,128)(2,1)}, bf16[2,1,512,512]{3,2,1,0:T(8,128)(2,1)S(1)}, u32[]{:S(2)}, u32[]{:S(2)}) collective-permute-start(bf16[2,1,512,512]{3,2,1,0:T(8,128)(2,1)} %get-tuple-element.93), channel_id=1, source_target_pairs={{0,8},{8,0},{16,24},{24,16},{1,9},{9,1},{17,25},{25,17},{2,10},{10... | collective-permute-start | bytes 3145736 | tf_op jit(solution)/shard_map/ppermute | solution.py:21
  125.3 25.7 %collective-permute-start.25 = (bf16[2,1,512,512]{3,2,1,0:T(8,128)(2,1)}, bf16[2,1,512,512]{3,2,1,0:T(8,128)(2,1)S(1)}, u32[]{:S(2)}, u32[]{:S(2)}) collective-permute-start(bf16[2,1,512,512]{3,2,1,0:T(8,128)(2,1)} %get-tuple-element.99), channel_id=1, source_target_pairs={{0,16},{8,24},{16,0},{24,8},{1,17},{9,25},{17,1},{25,9},{2,18},{10... | collective-permute-start | bytes 3145736 | tf_op jit(solution)/shard_map/ppermute | solution.py:21
  125.8 32.0 %collective-permute-start.27 = (bf16[2,512,512]{2,1,0:T(8,128)(2,1)}, bf16[2,512,512]{2,1,0:T(8,128)(2,1)S(1)}, u32[]{:S(2)}, u32[]{:S(2)}) collective-permute-start(bf16[2,512,512]{2,1,0:T(8,128)(2,1)} %get-tuple-element.101), channel_id=1, source_target_pairs={{0,2},{1,3},{2,0},{3,1},{4,6},{5,7},{6,4},{7,5},{8,10},{9,11},{10,... | collective-permute-start | bytes 3145736 | tf_op jit(solution)/shard_map/ppermute | solution.py:21
  142.5 11.0 %collective-permute-start.23 = (bf16[256,8]{1,0:T(8,128)(2,1)S(1)}, bf16[256,8]{1,0:T(8,128)(2,1)S(1)}, u32[]{:S(2)}, u32[]{:S(2)}) collective-permute-start(bf16[256,8]{1,0:T(8,128)(2,1)S(1)} %pad_maximum_fusion), channel_id=1, source_target_pairs={{0,1},{1,0},{2,3},{3,2},{4,5},{5,4},{6,7},{7,6},{8,9},{9,8},{10,11... | collective-permute-start | bytes 12296 | tf_op jit(solution)/shard_map/ppermute | solution.py:21
  144.1 33.7 %collective-permute-start.21 = (bf16[128,2048]{1,0:T(8,128)(2,1)}, bf16[128,2048]{1,0:T(8,128)(2,1)}, u32[]{:S(2)}, u32[]{:S(2)}) collective-permute-start(bf16[128,2048]{1,0:T(8,128)(2,1)} %get-tuple-element.95), channel_id=1, source_target_pairs={{0,1},{1,0},{2,3},{3,2},{4,5},{5,4},{6,7},{7,6},{8,9},{9,8},{10,11... | collective-permute-start | bytes 1572872 | tf_op jit(solution)/shard_map/ppermute | solution.py:21
  144.6 33.2 %collective-permute-start.22 = (bf16[128,2048]{1,0:T(8,128)(2,1)}, bf16[128,2048]{1,0:T(8,128)(2,1)}, u32[]{:S(2)}, u32[]{:S(2)}) collective-permute-start(bf16[128,2048]{1,0:T(8,128)(2,1)} %get-tuple-element.96), channel_id=1, source_target_pairs={{0,4},{1,5},{2,6},{3,7},{4,0},{5,1},{6,2},{7,3},{8,12},{9,13},{10,... | collective-permute-start | bytes 1572872 | tf_op jit(solution)/shard_map/ppermute | solution.py:21
  153.4 21.1 %collective-permute-start.26 = (bf16[512,512]{1,0:T(8,128)(2,1)}, bf16[512,512]{1,0:T(8,128)(2,1)}, u32[]{:S(2)}, u32[]{:S(2)}) collective-permute-start(bf16[512,512]{1,0:T(8,128)(2,1)} %slice_bitcast_fusion), channel_id=1, source_target_pairs={{0,2},{1,3},{2,0},{3,1},{4,6},{5,7},{6,4},{7,5},{8,10},{9,11},{10,... | collective-permute-start | bytes 1572872 | tf_op jit(solution)/shard_map/ppermute | solution.py:21
  153.5 18.8 %collective-permute-start.24 = (bf16[128,8]{1,0:T(8,128)(2,1)S(1)}, bf16[128,8]{1,0:T(8,128)(2,1)S(1)}, u32[]{:S(2)}, u32[]{:S(2)}) collective-permute-start(bf16[128,8]{1,0:T(8,128)(2,1)S(1)} %add_convert_fusion.9), channel_id=1, source_target_pairs={{0,4},{1,5},{2,6},{3,7},{4,0},{5,1},{6,2},{7,3},{8,12},{9,13},{10,... | collective-permute-start | bytes 6152 | tf_op jit(solution)/shard_map/ppermute | solution.py:21
  158.1 18.5 %collective-permute-start.28 = (bf16[1,512,512]{2,1,0:T(8,128)(2,1)S(1)}, bf16[1,512,512]{2,1,0:T(8,128)(2,1)S(1)}, u32[]{:S(2)}, u32[]{:S(2)}) collective-permute-start(bf16[1,512,512]{2,1,0:T(8,128)(2,1)S(1)} %slice.19), channel_id=1, source_target_pairs={{0,16},{8,24},{16,0},{24,8},{1,17},{9,25},{17,1},{25,9},{2,18},{10... | collective-permute-start | bytes 1572872 | tf_op jit(solution)/shard_map/ppermute | solution.py:21
  (24 other events, 65.3 us)
